TPU v7x, 256 devices: a whole 4x4x8 slice. The times are simulated.
256 devices in a mesh: cache: 32 (over x, z), tensor: 8 (over y, core).
Axes of the slice: x: 4, y: 4, z: 8, core: 2. Of those that a mesh axis runs over, the one named last changes fastest.
Arguments:
- queries: bfloat16 [1024, 32, 8192], P('cache', None, 'tensor'), may hold values from -18 to 18
- prefix_kv: bfloat16 [2, 32, 512, 1024], P(None, 'cache', None, 'tensor'), may hold values from -12 to 12
- suffix_kv: bfloat16 [2, 1024, 32, 1024], P(None, 'cache', None, 'tensor'), may hold values from -12 to 12
- candidate_prefix: int32 [1024, 1], P('cache'), may hold values from 0 to 31; in each aligned block of 32 rows (0 to 31, 32 to 63, ...) at most 2 rows name the same one
- w_out: bfloat16 [8192, 4096], P('tensor'), may hold values from -1 to 1
Outputs:
- projected: bfloat16 [1024, 32, 4096], P('cache', None, 'tensor')
Inputs may be any that keep to these rules, and one draw needn't show every extreme that they name: `candidate_prefix`: the passage with id p has its cache at prefix_kv[:, p]. Among the candidates of one index of cache at most 2 name the same passage, and exactly 2 do for some passage in some of them.
All inputs are finite; a program needn't handle non-finite values.
Results may differ from a plain program's by a relative error of at most 0.019.
Values may be sent and summed in bfloat16 or wider, within the bound.
No kernel may reach another device: no remote copies, remote signals or barrier semaphores. Data moves between devices by JAX's collectives and lax.ppermute only.
A program may use at most 128 MiB of HBM per device.

v0:
```python
import functools
import math

import jax
import jax.numpy as jnp
from jax import lax
from jax.experimental import pallas as pl
from jax.experimental.pallas import tpu as pltpu
from jax.sharding import PartitionSpec as P

H = 64
KVH = 8
HD = 128
GROUP = H // KVH
NX = 4
NZ = 8
NY = 4
LATE = 9
LOG2E = 1.4426950408889634
MIB = 1024 * 1024


def send_cache(value, along_z):
    pairs = []
    for x in range(NX):
        for z in range(NZ):
            for t in range(2 * NY):
                step = -1 if t % 2 else 1
                to_x, to_z = (x, (z + step) % NZ) if along_z else ((x + step) % NX, z)
                pairs.append(((x * NZ + z) * 2 * NY + t, (to_x * NZ + to_z) * 2 * NY + t))
    return lax.ppermute(value, ("cache", "tensor"), pairs)


def send_y(value, step):
    pairs = [(2 * y + c, 2 * ((y + step) % NY) + c) for y in range(NY) for c in range(2)]
    return lax.ppermute(value, "tensor", pairs)


def swap_core(value):
    return lax.ppermute(value, "tensor", [(t, t ^ 1) for t in range(2 * NY)])


def together(*values):
    return lax.optimization_barrier(values)


def pack_kernel(places, n_arrays, *refs):
    o_ref = refs[n_arrays]
    for index, (which, at) in places:
        o_ref[index] = refs[which][at]


def pack(parts):
    arrays = []
    places = []
    for i, row in enumerate(parts):
        for j, (array, at) in enumerate(row):
            which = next((n for n, a in enumerate(arrays) if a is array), len(arrays))
            if which == len(arrays):
                arrays.append(array)
            places.append(((i, j), (which, at)))
    block = arrays[0].shape[-2:]
    vmem = pl.BlockSpec(memory_space=pltpu.VMEM)
    return pl.pallas_call(
        functools.partial(pack_kernel, places, len(arrays)),
        out_shape=jax.ShapeDtypeStruct((len(parts), len(parts[0])) + block, jnp.bfloat16),
        in_specs=[vmem] * len(arrays),
        out_specs=vmem,
        compiler_params=pltpu.CompilerParams(vmem_limit_bytes=6 * MIB),
        cost_estimate=pl.CostEstimate(flops=0, bytes_accessed=MIB, transcendentals=0),
    )(*arrays)


class Gather:
    def __init__(self, block):
        self.block = block
        self.sources = {}

    def part(self, array, at, kv, dz, dx):
        code = (dz % NZ) * NX + dx % NX
        self.sources.setdefault(code, []).append((array, at, kv))

    def whole(self, array, at, dz, dx):
        for kv in range(2):
            self.part(array, at + (kv,), kv, dz, dx)

    def early(self, *tokens):
        block = self.block
        other = swap_core(block)
        both = pack([[(block, 0), (block, 1)], [(other, 0), (other, 1)]])
        x1, z1 = send_cache(both, False), send_cache(both, True)
        x1, z1, *tokens = together(x1, z1, *tokens)
        x1m, z1m = swap_core(x1), swap_core(z1)
        x2, z2 = send_cache(x1, False), send_cache(z1, True)
        x2, z2, x1m, z1m = together(x2, z2, x1m, z1m)
        values = pack(
            [
                [(x1, (0, 1)), (x1m, (1, 1)), (x2, (0, 1))],
                [(x1, (1, 1)), (x1m, (0, 1)), (x2, (1, 1))],
            ]
        )
        z2m = swap_core(z2)
        near = pack(
            [
                [(z1, (0, 0)), (z1m, (1, 0)), (z2, (0, 0)), (z2m, (1, 0))],
                [(z1, (1, 0)), (z1m, (0, 0)), (z2, (1, 0)), (z2m, (0, 0))],
            ]
        )
        v1, n1 = send_cache(values, True), send_cache(near, False)
        z3 = send_cache(z2, True)
        v1, n1, z3 = together(v1, n1, z3)
        z3m, n1m, v1m = swap_core(z3), swap_core(n1[1]), swap_core(v1[1])
        z4, n2, v2 = send_cache(z3[0], True), send_cache(n1[0], False), send_cache(v1, True)
        z4, n2, v2, z3m, n1m, v1m = together(z4, n2, v2, z3m, n1m, v1m)
        v2m = swap_core(v2[1])

        self.whole(block, (), 0, 0)
        self.whole(x1, (0,), 0, 1)
        self.whole(x1m, (1,), 0, -1)
        self.whole(x2, (0,), 0, 2)
        for step, mine, mate in ((1, z1, z1m), (2, z2, z2m), (3, z3, z3m)):
            self.whole(mine, (0,), step, 0)
            self.whole(mate, (1,), -step, 0)
        self.whole(z4, (), 4, 0)
        for step, mine, mate in ((1, v1, v1m), (2, v2, v2m)):
            self.values(mine, mate, step)
        for at, dz in enumerate((1, -1, 2, -2)):
            self.part(n1, (0, at), 0, dz, 1)
            self.part(n1m, (at,), 0, -dz, -1)
            self.part(n2, (at,), 0, dz, 2)
        self.left = v2, z3, z3m, z4
        return tokens, {code: list(parts) for code, parts in self.sources.items()}

    def values(self, mine, mate, step):
        for at, dx in enumerate((1, -1, 2)):
            self.part(mine, (0, at), 1, step, dx)
            self.part(mate, (at,), 1, -step, -dx)

    def late(self):
        v2, z3, z3m, z4 = self.left
        key_z4m = swap_core(z4[0:1])
        distant = pack(
            [
                [(z3, (0, 0)), (z3m, (1, 0)), (z4, 0)],
                [(z3, (1, 0)), (z3m, (0, 0)), (key_z4m, 0)],
            ]
        )
        self.hop = send_cache(v2, True), send_cache(distant, False)

    def last(self, token):
        token, v3, f1 = together(token, *self.hop)
        v4, f2 = send_cache(v3[0], True), send_cache(f1[0], False)
        self.final = v3, f1, v4, f2
        return token

    def finish(self, *tokens):
        count = len(tokens)
        done = together(*tokens, *self.final)
        v3, f1, v4, f2 = done[count:]
        third = range(3)
        rest = swap_core(pack([[(v3, (1, at)) for at in third], [(f1, (1, at)) for at in third]]))
        for at, dx in enumerate((1, -1, 2)):
            self.part(v3, (0, at), 1, 3, dx)
            self.part(rest, (0, at), 1, -3, -dx)
            self.part(v4, (at,), 1, 4, dx)
        for at, dz in enumerate((3, -3, 4)):
            self.part(f1, (0, at), 0, dz, 1)
            self.part(rest, (1, at), 0, -dz, -1)
            self.part(f2, (at,), 0, dz, 2)
        return done[:count], self.sources


LAST = (((1,), (1,)), ((), ()))
INNER = (((1,), (0,)), ((), ()))


def beside_ones(values):
    return jnp.concatenate([values, jnp.ones_like(values)], axis=1)


def plan_kernel(ids, order, codes, info):
    me = lax.axis_index("cache")
    t = lax.axis_index("tensor")
    count = ids.shape[0]
    info[0] = t // 2
    info[1] = t % 2

    def is_early(code):
        dz = code // NX
        return (code % NX == 0) | (dz <= 2) | (dz >= NZ - 2)

    def first(n, at):
        passage = ids[n]
        dz = (passage % NZ - me % NZ + NZ) % NZ
        dx = (passage // NZ - me // NZ + NX) % NX
        dz = jnp.where(t % 2 == 0, (NZ - dz) % NZ, dz)
        dx = jnp.where(t % 2 == 0, (NX - dx) % NX, dx)
        code = dz * NX + dx
        codes[n] = code
        order[at] = n
        return at + is_early(code).astype(jnp.int32)

    early = lax.fori_loop(0, count, first, jnp.int32(0))

    def second(n, at):
        late = jnp.logical_not(is_early(codes[n]))

        @pl.when(late)
        def _():
            order[at] = n

        return at + late.astype(jnp.int32)

    lax.fori_loop(0, count, second, early)


def plan(candidate_prefix):
    count = candidate_prefix.shape[0]
    smem = pl.BlockSpec(memory_space=pltpu.SMEM)
    return pl.pallas_call(
        plan_kernel,
        out_shape=[jax.ShapeDtypeStruct((n,), jnp.int32) for n in (count, count, 2)],
        in_specs=[smem],
        out_specs=[smem] * 3,
        compiler_params=pltpu.CompilerParams(vmem_limit_bytes=MIB),
        cost_estimate=pl.CostEstimate(flops=1000, bytes_accessed=1000, transcendentals=0),
    )(candidate_prefix.reshape(count))


def attention_kernel(sources, n_arrays, lo, count, batch, order, codes, q_ref, s_ref, *rest):
    arrays = rest[:n_arrays]
    o_ref, cache = rest[n_arrays:]
    suffix = q_ref.shape[1]
    rows = GROUP * suffix
    factor = LOG2E / math.sqrt(HD)
    token = lax.broadcasted_iota(jnp.int32, (rows, HD), 0) % suffix
    causal = lax.broadcasted_iota(jnp.int32, (rows, HD), 1) <= token
    blank = jnp.zeros((HD - suffix, HD), jnp.bfloat16)

    def fetch(first):
        @pl.loop(0, batch)
        def _(i):
            code = codes[order[first + i]]
            for dx in range(NX):

                @pl.when(code % NX == dx)
                def _(dx=dx):
                    for dz in range(NZ):
                        parts = sources.get(dz * NX + dx)
                        if parts is None:
                            continue

                        @pl.when(code // NX == dz)
                        def _(parts=parts):
                            for which, at, kv in parts:
                                cache[i, kv] = arrays[which][at]

    def attend_batch(first, at):
        fetch(first)
        scores = []
        for i in range(batch):
            n = order[first + i]
            q = jnp.concatenate([q_ref[n, :, g * HD : (g + 1) * HD] for g in range(GROUP)], axis=0)
            far = lax.dot_general(q, cache[i, 0], LAST, preferred_element_type=jnp.float32)
            keys = jnp.concatenate([s_ref[0, n], blank], axis=0)
            near = lax.dot_general(q, keys, LAST, preferred_element_type=jnp.float32)
            near = jnp.where(causal, near, -jnp.inf)
            scores.append([far[:, j : j + HD] for j in range(0, far.shape[1], HD)] + [near])
        weights = []
        for tiles in scores:
            top = jnp.max(functools.reduce(jnp.maximum, tiles), axis=1, keepdims=True)
            weights.append([jnp.exp2((s - top) * factor).astype(jnp.bfloat16) for s in tiles])
        for i in range(batch):
            n = order[first + i]
            far = jnp.concatenate(weights[i][:-1], axis=1)
            near = weights[i][-1][:, :suffix]
            summed = lax.dot_general(
                far, beside_ones(cache[i, 1]), INNER, preferred_element_type=jnp.float32
            ) + lax.dot_general(
                near, beside_ones(s_ref[1, n]), INNER, preferred_element_type=jnp.float32
            )
            result = (summed[:, :HD] / summed[:, HD:]).astype(jnp.bfloat16)
            for g in range(GROUP):
                o_ref[at + i, :, g * HD : (g + 1) * HD] = result[g * suffix : (g + 1) * suffix]

    @pl.loop(0, -(-count // batch))
    def _(step):
        at = jnp.minimum(step * batch, count - batch)
        attend_batch(lo + at, at)


def attend(order, codes, queries, suffix_kv, sources, lo, count, length):
    arrays = []
    places = {}
    for code, parts in sources.items():
        for array, at, kv in parts:
            which = next((n for n, a in enumerate(arrays) if a is array), len(arrays))
            if which == len(arrays):
                arrays.append(array)
            places.setdefault(code, []).append((which, at, kv))
    _, suffix, width = queries.shape
    batch = 4
    vmem = pl.BlockSpec(memory_space=pltpu.VMEM)
    smem = pl.BlockSpec(memory_space=pltpu.SMEM)
    shape = jax.ShapeDtypeStruct((count, suffix, width), jnp.bfloat16)
    return pl.pallas_call(
        functools.partial(attention_kernel, places, len(arrays), lo, count, batch),
        out_shape=shape,
        in_specs=[smem] * 2 + [vmem] * (2 + len(arrays)),
        out_specs=vmem,
        scratch_shapes=[pltpu.VMEM((batch, 2, length, HD), jnp.bfloat16)],
        compiler_params=pltpu.CompilerParams(vmem_limit_bytes=28 * MIB),
        cost_estimate=pl.CostEstimate(
            flops=4 * count * suffix * width * length,
            bytes_accessed=8 * MIB,
            transcendentals=count * suffix * GROUP * length,
        ),
    )(order, codes, queries, suffix_kv, *arrays)


def columns_of(place, turn, other, width):
    core = 1 - place[1] if other else place[1]
    return pl.multiple_of((2 * lax.rem(place[0] + turn, NY) + core) * width, width)


def project_other_kernel(turns, place, a_ref, w_ref, o_ref):
    width = o_ref.shape[2]
    for at, turn in enumerate(turns):
        column = columns_of(place, turn, True, width)
        total = jnp.dot(
            a_ref[...], w_ref[:, pl.ds(column, width)], preferred_element_type=jnp.float32
        )
        o_ref[at] = total.astype(jnp.bfloat16)


def project_own_kernel(turns, first, split, place, a_ref, w_ref, came_ref, *outs):
    width = came_ref.shape[2]
    half = a_ref.shape[0] // 2
    for at, turn in enumerate(turns):
        column = columns_of(place, turn, False, width)
        total = jnp.dot(
            a_ref[...], w_ref[:, pl.ds(column, width)], preferred_element_type=jnp.float32
        )
        total = (total + came_ref[first + at].astype(jnp.float32)).astype(jnp.bfloat16)
        if split:
            outs[2 * at][...] = total[:half]
            outs[2 * at + 1][...] = total[half:]
        else:
            outs[at][...] = total


def project(kernel, out_shape, place, *arrays):
    vmem = pl.BlockSpec(memory_space=pltpu.VMEM)
    rows, depth = arrays[0].shape
    outs = out_shape if isinstance(out_shape, list) else [out_shape]
    size = sum(math.prod(out.shape) for out in outs)
    return pl.pallas_call(
        kernel,
        out_shape=out_shape,
        in_specs=[pl.BlockSpec(memory_space=pltpu.SMEM)] + [vmem] * len(arrays),
        out_specs=[vmem] * len(outs) if isinstance(out_shape, list) else vmem,
        compiler_params=pltpu.CompilerParams(vmem_limit_bytes=20 * MIB),
        cost_estimate=pl.CostEstimate(
            flops=2 * size * depth, bytes_accessed=4 * MIB, transcendentals=0
        ),
    )(place, *arrays)


def project_other(place, mine, w_out, turns, width):
    shape = jax.ShapeDtypeStruct((len(turns), mine.shape[0], width), jnp.bfloat16)
    return project(functools.partial(project_other_kernel, turns), shape, place, mine, w_out)


def project_own(place, mine, w_out, turns, came, first, split=False):
    parts = 2 if split else 1
    shape = jax.ShapeDtypeStruct((mine.shape[0] // parts, came.shape[2]), jnp.bfloat16)
    kernel = functools.partial(project_own_kernel, turns, first, split)
    return project(kernel, [shape] * (parts * len(turns)), place, mine, w_out, came)


def merge_kernel(up, down, top, low, up_out, down_out):
    half = top.shape[0]
    up_out[:half] = (up[:half].astype(jnp.float32) + top[...]).astype(jnp.bfloat16)
    up_out[half:] = up[half:]
    down_out[:half] = down[:half]
    down_out[half:] = (down[half:].astype(jnp.float32) + low[...]).astype(jnp.bfloat16)


def merge(up, down, top, low):
    vmem = pl.BlockSpec(memory_space=pltpu.VMEM)
    return pl.pallas_call(
        merge_kernel,
        out_shape=[jax.ShapeDtypeStruct(up.shape, up.dtype)] * 2,
        in_specs=[vmem] * 4,
        out_specs=[vmem] * 2,
        compiler_params=pltpu.CompilerParams(vmem_limit_bytes=8 * MIB),
        cost_estimate=pl.CostEstimate(flops=0, bytes_accessed=MIB, transcendentals=0),
    )(up, down, top, low)


def final_kernel(suffix, chunks, order, *refs):
    o_ref = refs[-1]
    for lo, at in chunks:
        terms = refs[at : at + 3]

        @pl.loop(0, terms[0].shape[0] // suffix)
        def _(n, lo=lo, terms=terms):
            here = pl.ds(pl.multiple_of(n * suffix, suffix), suffix)
            total = sum(term[here].astype(jnp.float32) for term in terms)
            o_ref[order[lo + n]] = total.astype(jnp.bfloat16)


class Projection:
    def __init__(self, place, w_out, mine, width, *tokens):
        near = project_other(place, mine, w_out, (2,), width)
        near, *self.tokens = together(near, *tokens)
        self.near = swap_core(near)
        self.project = functools.partial(project_own, place, mine, w_out)
        top2, low2 = self.project((2,), self.near, 0, True)
        later, self.top2, self.low2 = together(mine, top2, low2)
        self.rest = swap_core(project_other(place, later, w_out, (1, 3, 0), width))

    def across(self):
        return send_y(self.top2, 1), send_y(self.low2, -1)

    def beside(self):
        return self.project((1, 3), self.rest, 0)

    def own(self):
        return self.project((0,), self.rest, 2)[0]


def shards(queries, prefix_kv, suffix_kv, candidate_prefix, w_out):
    count, suffix, width = queries.shape
    length = prefix_kv.shape[2]
    out_width = w_out.shape[1] // (2 * NY)
    chunk = count - 2 * LATE
    others = count - chunk
    order, codes, info = plan(candidate_prefix)

    gather = Gather(prefix_kv.reshape(2, length, HD))
    (order, codes, info), sources = gather.early(order, codes, info)

    mine = attend(order, codes, queries, suffix_kv, sources, 0, chunk, length)
    gather.late()
    mine = gather.last(mine.reshape(chunk * suffix, width))
    one = Projection(info, w_out, mine, out_width)
    top2, low2 = one.across()
    up, down = one.beside()
    (up, down, top2, low2, order2), sources = gather.finish(up, down, top2, low2, order)
    up, down = merge(up, down, top2, low2)
    up, down = send_y(up, 1), send_y(down, -1)

    mine = attend(order2, codes, queries, suffix_kv, sources, chunk, others, length)
    two = Projection(info, w_out, mine.reshape(others * suffix, width), out_width, up, down)
    up, down = two.tokens
    terms = [one.own(), up, down]
    top2, low2 = two.across()
    up, down = two.beside()
    up, down = merge(up, down, top2, low2)
    terms += [two.own(), send_y(up, 1), send_y(down, -1)]
    return pl.pallas_call(
        functools.partial(final_kernel, suffix, [(0, 0), (chunk, 3)]),
        out_shape=jax.ShapeDtypeStruct((count, suffix, out_width), jnp.bfloat16),
        in_specs=[pl.BlockSpec(memory_space=pltpu.SMEM)]
        + [pl.BlockSpec(memory_space=pltpu.VMEM)] * 6,
        out_specs=pl.BlockSpec(memory_space=pltpu.VMEM),
        compiler_params=pltpu.CompilerParams(vmem_limit_bytes=12 * MIB),
    )(order, *terms)


def solution(mesh):
    in_specs = (
        P("cache", None, "tensor"),
        P(None, "cache", None, "tensor"),
        P(None, "cache", None, "tensor"),
        P("cache", None),
        P("tensor", None),
    )
    out_specs = P("cache", None, "tensor")
    return jax.shard_map(shards, mesh=mesh, in_specs=in_specs, out_specs=out_specs, check_vma=False)
```

profile of v0, /device:TPU:1, one launch (start us, length us, event | category | flops | bytes accessed | tf_op | source)
XLA Modules:
  0.0 148.6 jit_solution(7897501064638928042)
XLA Ops:
  0.0 3.2 %collective-permute-start = (bf16[2,512,128]{2,1,0:T(8,128)(2,1)}, bf16[2,512,128]{2,1,0:T(8,128)(2,1)S(1)}, u32[]{:S(2)}, u32[]{:S(2)}) collective-permute-start(bf16[2,512,128]{2,1,0:T(8,128)(2,1)} %bitcast.30), channel_id=1, source_target_pairs={{0,1},{1,0},{2,3},{3,2},{4,5},{5,4},{6,7},{7,6},{8,9},{9,8},{10,11... | collective-permute-start | bytes 786440 | tf_op jit(solution)/shard_map/ppermute | solution.py:40
  6.4 5.6 %collective-permute-start.2 = (bf16[2,2,512,128]{3,2,1,0:T(8,128)(2,1)S(1)}, bf16[2,2,512,128]{3,2,1,0:T(8,128)(2,1)S(1)}, u32[]{:S(2)}, u32[]{:S(2)}) collective-permute-start(bf16[2,2,512,128]{3,2,1,0:T(8,128)(2,1)S(1)} %shard_map.55), channel_id=1, source_target_pairs={{0,8},{1,57},{2,10},{3,59},{4,12},{5,61},{6,14},{7,63},{8,16},{9,1... | collective-permute-start | bytes 1572872 | tf_op jit(solution)/shard_map/ppermute | solution.py:31
  12.7 2.9 %shard_map.56 = (s32[32]{0:T(128)S(1)}, s32[32]{0:T(128)S(1)}, s32[2]{0:T(128)S(1)}) custom-call(s32[32]{0:T(128)S(1)} %bitcast.34), custom_call_target="tpu_custom_call" | custom-call | flops 1000 | bytes 1000 | tf_op jit(solution)/shard_map/pallas_call | solution.py:220
  15.6 2.5 %collective-permute-done.2.refs_0_.rest_4_ = bf16[2,2,512,128]{3,2,1,0:T(8,128)(2,1)S(1)} collective-permute-done((bf16[2,2,512,128]{3,2,1,0:T(8,128)(2,1)S(1)}, bf16[2,2,512,128]{3,2,1,0:T(8,128)(2,1)S(1)}, u32[]{:S(2)}, u32[]{:S(2)}) %collective-permute-start.2) | collective-permute-done | bytes 524320 | tf_op jit(solution)/shard_map/ppermute | solution.py:31
  18.7 3.1 %collective-permute-start.4 = (bf16[2,2,512,128]{3,2,1,0:T(8,128)(2,1)S(1)}, bf16[2,2,512,128]{3,2,1,0:T(8,128)(2,1)S(1)}, u32[]{:S(2)}, u32[]{:S(2)}) collective-permute-start(bf16[2,2,512,128]{3,2,1,0:T(8,128)(2,1)S(1)} %collective-permute-done.2.refs_0_.rest_4_), channel_id=1, source_target_pairs={{0,8},{1,57},{2,10},{3,59},{4,12},{5,61},{6,14},{7,63},{8,16},{9,1... | collective-permute-start | bytes 1572872 | tf_op jit(solution)/shard_map/ppermute | solution.py:31
  22.3 4.2 %collective-permute-done.3.refs_2_.rest_3_ = bf16[2,2,512,128]{3,2,1,0:T(8,128)(2,1)S(1)} collective-permute-done((bf16[2,2,512,128]{3,2,1,0:T(8,128)(2,1)S(1)}, bf16[2,2,512,128]{3,2,1,0:T(8,128)(2,1)S(1)}, u32[]{:S(2)}, u32[]{:S(2)}) %collective-permute-start.3) | collective-permute-done | bytes 524320 | tf_op jit(solution)/shard_map/ppermute | solution.py:31
  27.9 2.8 %collective-permute-start.7 = (bf16[2,2,512,128]{3,2,1,0:T(8,128)(2,1)S(1)}, bf16[2,2,512,128]{3,2,1,0:T(8,128)(2,1)S(1)}, u32[]{:S(2)}, u32[]{:S(2)}) collective-permute-start(bf16[2,2,512,128]{3,2,1,0:T(8,128)(2,1)S(1)} %collective-permute-done.4.refs_2_.rest_6_), channel_id=1, source_target_pairs={{0,1},{1,0},{2,3},{3,2},{4,5},{5,4},{6,7},{7,6},{8,9},{9,8},{10,11... | collective-permute-start | bytes 1572872 | tf_op jit(solution)/shard_map/ppermute | solution.py:40
  35.3 15.5 %collective-permute-done.10.rest_8_.refs_0_ = bf16[2,2,512,128]{3,2,1,0:T(8,128)(2,1)S(1)} collective-permute-done((bf16[2,2,512,128]{3,2,1,0:T(8,128)(2,1)S(1)}, bf16[2,2,512,128]{3,2,1,0:T(8,128)(2,1)S(1)}, u32[]{:S(2)}, u32[]{:S(2)}) %collective-permute-start.10) | collective-permute-done | bytes 524320 | tf_op jit(solution)/shard_map/ppermute | solution.py:31
  50.8 2.3 %collective-permute-start.14 = (bf16[2,2,512,128]{3,2,1,0:T(8,128)(2,1)S(1)}, bf16[2,2,512,128]{3,2,1,0:T(8,128)(2,1)S(1)}, u32[]{:S(2)}, u32[]{:S(2)}) collective-permute-start(bf16[2,2,512,128]{3,2,1,0:T(8,128)(2,1)S(1)} %collective-permute-done.10.rest_8_.refs_0_), channel_id=1, source_target_pairs={{0,1},{1,0},{2,3},{3,2},{4,5},{5,4},{6,7},{7,6},{8,9},{9,8},{10,11... | collective-permute-start | bytes 1572872 | tf_op jit(solution)/shard_map/ppermute | solution.py:40
  53.2 1.8 %collective-permute-start.12 = (bf16[4,512,128]{2,1,0:T(8,128)(2,1)S(1)}, bf16[4,512,128]{2,1,0:T(8,128)(2,1)S(1)}, u32[]{:S(2)}, u32[]{:S(2)}) collective-permute-start(bf16[4,512,128]{2,1,0:T(8,128)(2,1)S(1)} %get-tuple-element.114), channel_id=1, source_target_pairs={{0,64},{1,193},{2,66},{3,195},{4,68},{5,197},{6,70},{7,199},{8,72}... | collective-permute-start | bytes 1572872 | tf_op jit(solution)/shard_map/ppermute | solution.py:31
  55.1 3.5 %collective-permute-done.11.rest_10_.refs_2_ = bf16[2,512,128]{2,1,0:T(8,128)(2,1)S(1)} collective-permute-done((bf16[2,512,128]{2,1,0:T(8,128)(2,1)S(1)}, bf16[2,512,128]{2,1,0:T(8,128)(2,1)S(1)}, u32[]{:S(2)}, u32[]{:S(2)}) %collective-permute-start.11) | collective-permute-done | bytes 262176 | tf_op jit(solution)/shard_map/ppermute | solution.py:31
  58.6 2.2 %collective-permute-start.16 = (bf16[3,512,128]{2,1,0:T(8,128)(2,1)S(1)}, bf16[3,512,128]{2,1,0:T(8,128)(2,1)S(1)}, u32[]{:S(2)}, u32[]{:S(2)}) collective-permute-start(bf16[3,512,128]{2,1,0:T(8,128)(2,1)S(1)} %slice_bitcast_fusion.5), channel_id=1, source_target_pairs={{0,1},{1,0},{2,3},{3,2},{4,5},{5,4},{6,7},{7,6},{8,9},{9,8},{10,11... | collective-permute-start | bytes 1179656 | tf_op jit(solution)/shard_map/ppermute | solution.py:40
  62.1 4.9 %collective-permute-done.13.rest_16_ = bf16[2,3,512,128]{3,2,1,0:T(8,128)(2,1)S(1)} collective-permute-done((bf16[2,3,512,128]{3,2,1,0:T(8,128)(2,1)S(1)}, bf16[2,3,512,128]{3,2,1,0:T(8,128)(2,1)S(1)}, u32[]{:S(2)}, u32[]{:S(2)}) %collective-permute-start.13) | collective-permute-done | bytes 786464 | tf_op jit(solution)/shard_map/ppermute | solution.py:31
  67.0 2.4 %collective-permute-start.19 = (bf16[1,512,128]{2,1,0:T(8,128)(2,1)S(1)}, bf16[1,512,128]{2,1,0:T(8,128)(2,1)S(1)}, u32[]{:S(2)}, u32[]{:S(2)}) collective-permute-start(bf16[1,512,128]{2,1,0:T(8,128)(2,1)S(1)} %slice.29), channel_id=1, source_target_pairs={{0,1},{1,0},{2,3},{3,2},{4,5},{5,4},{6,7},{7,6},{8,9},{9,8},{10,11... | collective-permute-start | bytes 393224 | tf_op jit(solution)/shard_map/ppermute | solution.py:40
  70.5 1.8 %collective-permute-start.20 = (bf16[2,3,512,128]{3,2,1,0:T(8,128)(2,1)S(1)}, bf16[2,3,512,128]{3,2,1,0:T(8,128)(2,1)S(1)}, u32[]{:S(2)}, u32[]{:S(2)}) collective-permute-start(bf16[2,3,512,128]{3,2,1,0:T(8,128)(2,1)S(1)} %shard_map.60), channel_id=1, source_target_pairs={{0,64},{1,193},{2,66},{3,195},{4,68},{5,197},{6,70},{7,199},{8,72}... | collective-permute-start | bytes 2359304 | tf_op jit(solution)/shard_map/ppermute | solution.py:31
  72.5 1.7 %collective-permute-done.17.rest_17_ = bf16[3,512,128]{2,1,0:T(8,128)(2,1)S(1)} collective-permute-done((bf16[3,512,128]{2,1,0:T(8,128)(2,1)S(1)}, bf16[3,512,128]{2,1,0:T(8,128)(2,1)S(1)}, u32[]{:S(2)}, u32[]{:S(2)}) %collective-permute-start.17) | collective-permute-done | bytes 393248 | tf_op jit(solution)/shard_map/ppermute | solution.py:40
  74.2 6.4 %shard_map.59 = bf16[14,32,1024]{2,1,0:T(8,128)(2,1)S(1)} custom-call(s32[32]{0:T(128)S(1)} %get-tuple-element.90.order, s32[32]{0:T(128)S(1)} %get-tuple-element.64.codes, bf16[32,32,1024]{2,1,0:T(8,128)(2,1)S(1)} %copy-done, bf16[2,32,32,128]{3,2,1,0:T(8,128)(2,1)S(1)} %copy-done.3, bf16[2,512,128]{2,1,0:T(8,128)(2,1)S(1)} %bitcast.32, ...), custom_call_target="tpu_custom_call" | custom-call | flops 939524096 | bytes 8388608 | tf_op jit(solution)/shard_map/pallas_call | solution.py:306
  82.9 2.5 %collective-permute-start.21 = (bf16[1,448,512]{2,1,0:T(8,128)(2,1)S(1)}, bf16[1,448,512]{2,1,0:T(8,128)(2,1)S(1)}, u32[]{:S(2)}, u32[]{:S(2)}) collective-permute-start(bf16[1,448,512]{2,1,0:T(8,128)(2,1)S(1)} %shard_map.61), channel_id=1, source_target_pairs={{0,1},{1,0},{2,3},{3,2},{4,5},{5,4},{6,7},{7,6},{8,9},{9,8},{10,11... | collective-permute-start | bytes 1376264 | tf_op jit(solution)/shard_map/ppermute | solution.py:40
  88.0 2.1 %shard_map.63 = bf16[3,448,512]{2,1,0:T(8,128)(2,1)S(1)} custom-call(s32[2]{0:T(128)S(1)} %get-tuple-element.63.place, bf16[448,1024]{1,0:T(8,128)(2,1)S(1)} %bitcast.27, bf16[1024,4096]{1,0:T(8,128)(2,1)S(1)} %bitcast.19), custom_call_target="tpu_custom_call" | custom-call | flops 1409286144 | bytes 4194304 | tf_op jit(solution)/shard_map/pallas_call | solution.py:357
  90.7 1.8 %collective-permute-start.25 = (bf16[3,512,128]{2,1,0:T(8,128)(2,1)S(1)}, bf16[3,512,128]{2,1,0:T(8,128)(2,1)S(1)}, u32[]{:S(2)}, u32[]{:S(2)}) collective-permute-start(bf16[3,512,128]{2,1,0:T(8,128)(2,1)S(1)} %slice_bitcast_fusion.3), channel_id=1, source_target_pairs={{0,8},{1,57},{2,10},{3,59},{4,12},{5,61},{6,14},{7,63},{8,16},{9,1... | collective-permute-start | bytes 1179656 | tf_op jit(solution)/shard_map/ppermute | solution.py:31
  95.9 1.7 %shard_map.65 = (bf16[448,512]{1,0:T(8,128)(2,1)S(1)}, bf16[448,512]{1,0:T(8,128)(2,1)S(1)}) custom-call(s32[2]{0:T(128)S(1)} %get-tuple-element.63.place, bf16[448,1024]{1,0:T(8,128)(2,1)S(1)} %bitcast.28, bf16[1024,4096]{1,0:T(8,128)(2,1)S(1)} %bitcast.19, bf16[3,448,512]{2,1,0:T(8,128)(2,1)S(1)} %collective-permute-done.22.came_ref), custom_call_target="tpu_custom_call" | custom-call | flops 939524096 | bytes 4194304 | tf_op jit(solution)/shard_map/pallas_call | solution.py:357
  97.7 1.8 %collective-permute-done.26.rest_22_ = bf16[3,512,128]{2,1,0:T(8,128)(2,1)S(1)} collective-permute-done((bf16[3,512,128]{2,1,0:T(8,128)(2,1)S(1)}, bf16[3,512,128]{2,1,0:T(8,128)(2,1)S(1)}, u32[]{:S(2)}, u32[]{:S(2)}) %collective-permute-start.26) | collective-permute-done | bytes 393248 | tf_op jit(solution)/shard_map/ppermute | solution.py:31
  102.1 1.6 %collective-permute-start.29 = (bf16[448,512]{1,0:T(8,128)(2,1)S(1)}, bf16[448,512]{1,0:T(8,128)(2,1)S(1)}, u32[]{:S(2)}, u32[]{:S(2)}) collective-permute-start(bf16[448,512]{1,0:T(8,128)(2,1)S(1)} %get-tuple-element.100), channel_id=1, source_target_pairs={{0,6},{1,7},{2,0},{3,1},{4,2},{5,3},{6,4},{7,5},{8,14},{9,15},{10,... | collective-permute-start | bytes 1376264 | tf_op jit(solution)/shard_map/ppermute | solution.py:36
  103.7 8.0 %shard_map.67 = bf16[18,32,1024]{2,1,0:T(8,128)(2,1)S(1)} custom-call(s32[32]{0:T(128)S(1)} %get-tuple-element.90.order, s32[32]{0:T(128)S(1)} %get-tuple-element.64.codes, bf16[32,32,1024]{2,1,0:T(8,128)(2,1)S(1)} %copy-done, bf16[2,32,32,128]{3,2,1,0:T(8,128)(2,1)S(1)} %copy-done.3, bf16[2,512,128]{2,1,0:T(8,128)(2,1)S(1)} %bitcast.33, ...), custom_call_target="tpu_custom_call" | custom-call | flops 1207959552 | bytes 8388608 | tf_op jit(solution)/shard_map/pallas_call | solution.py:306
  115.1 1.6 %collective-permute-done.30.came_ref = bf16[1,576,512]{2,1,0:T(8,128)(2,1)S(1)} collective-permute-done((bf16[1,576,512]{2,1,0:T(8,128)(2,1)S(1)}, bf16[1,576,512]{2,1,0:T(8,128)(2,1)S(1)}, u32[]{:S(2)}, u32[]{:S(2)}) %collective-permute-start.30) | collective-permute-done | bytes 589856 | tf_op jit(solution)/shard_map/ppermute | solution.py:40
  118.0 2.5 %shard_map.71 = bf16[3,576,512]{2,1,0:T(8,128)(2,1)S(1)} custom-call(s32[2]{0:T(128)S(1)} %get-tuple-element.63.place, bf16[576,1024]{1,0:T(8,128)(2,1)S(1)} %bitcast.22, bf16[1024,4096]{1,0:T(8,128)(2,1)S(1)} %bitcast.19), custom_call_target="tpu_custom_call" | custom-call | flops 1811939328 | bytes 4194304 | tf_op jit(solution)/shard_map/pallas_call | solution.py:357
  122.1 1.8 %collective-permute-start.33 = (bf16[288,512]{1,0:T(8,128)(2,1)S(1)}, bf16[288,512]{1,0:T(8,128)(2,1)S(1)}, u32[]{:S(2)}, u32[]{:S(2)}) collective-permute-start(bf16[288,512]{1,0:T(8,128)(2,1)S(1)} %get-tuple-element.110), channel_id=1, source_target_pairs={{0,6},{1,7},{2,0},{3,1},{4,2},{5,3},{6,4},{7,5},{8,14},{9,15},{10,... | collective-permute-start | bytes 884744 | tf_op jit(solution)/shard_map/ppermute | solution.py:36
  124.4 1.9 %shard_map.73 = (bf16[576,512]{1,0:T(8,128)(2,1)S(1)}, bf16[576,512]{1,0:T(8,128)(2,1)S(1)}) custom-call(s32[2]{0:T(128)S(1)} %get-tuple-element.63.place, bf16[576,1024]{1,0:T(8,128)(2,1)S(1)} %bitcast.23, bf16[1024,4096]{1,0:T(8,128)(2,1)S(1)} %bitcast.19, bf16[3,576,512]{2,1,0:T(8,128)(2,1)S(1)} %collective-permute-done.31.came_ref), custom_call_target="tpu_custom_call" | custom-call | flops 1207959552 | bytes 4194304 | tf_op jit(solution)/shard_map/pallas_call | solution.py:357
  126.3 4.7 %collective-permute-done.32.top = bf16[288,512]{1,0:T(8,128)(2,1)S(1)} collective-permute-done((bf16[288,512]{1,0:T(8,128)(2,1)S(1)}, bf16[288,512]{1,0:T(8,128)(2,1)S(1)}, u32[]{:S(2)}, u32[]{:S(2)}) %collective-permute-start.32) | collective-permute-done | bytes 294944 | tf_op jit(solution)/shard_map/ppermute | solution.py:36
  131.7 2.2 %collective-permute-start.35 = (bf16[576,512]{1,0:T(8,128)(2,1)S(1)}, bf16[576,512]{1,0:T(8,128)(2,1)S(1)}, u32[]{:S(2)}, u32[]{:S(2)}) collective-permute-start(bf16[576,512]{1,0:T(8,128)(2,1)S(1)} %get-tuple-element.112), channel_id=1, source_target_pairs={{0,6},{1,7},{2,0},{3,1},{4,2},{5,3},{6,4},{7,5},{8,14},{9,15},{10,... | collective-permute-start | bytes 1769480 | tf_op jit(solution)/shard_map/ppermute | solution.py:36
  136.5 10.1 %collective-permute-done.34.refs_4_ = bf16[576,512]{1,0:T(8,128)(2,1)S(1)} collective-permute-done((bf16[576,512]{1,0:T(8,128)(2,1)S(1)}, bf16[576,512]{1,0:T(8,128)(2,1)S(1)}, u32[]{:S(2)}, u32[]{:S(2)}) %collective-permute-start.34) | collective-permute-done | bytes 589856 | tf_op jit(solution)/shard_map/ppermute | solution.py:36
  146.6 2.1 %shard_map.75 = bf16[32,32,512]{2,1,0:T(8,128)(2,1)} custom-call(s32[32]{0:T(128)S(1)} %get-tuple-element.90.order, bf16[448,512]{1,0:T(8,128)(2,1)S(1)} %shard_map.64.refs_0_, bf16[448,512]{1,0:T(8,128)(2,1)S(1)} %collective-permute-done.28.refs_1_, bf16[448,512]{1,0:T(8,128)(2,1)S(1)} %collective-permute-done.29.refs_2_, ...), custom_call_target="tpu_custom_call" | custom-call | tf_op jit(solution)/shard_map/pallas_call | solution.py:462
  (83 shorter events, 35.1 us)
Async XLA Ops:
  0.0 4.6 %collective-permute-start = (bf16[2,512,128]{2,1,0:T(8,128)(2,1)}, bf16[2,512,128]{2,1,0:T(8,128)(2,1)S(1)}, u32[]{:S(2)}, u32[]{:S(2)}) collective-permute-start(bf16[2,512,128]{2,1,0:T(8,128)(2,1)} %bitcast.30), channel_id=1, source_target_pairs={{0,1},{1,0},{2,3},{3,2},{4,5},{5,4},{6,7},{7,6},{8,9},{9,8},{10,11... | collective-permute-start | bytes 786440 | tf_op jit(solution)/shard_map/ppermute | solution.py:40
  5.6 10.0 %collective-permute-start.1 = (bf16[2,2,512,128]{3,2,1,0:T(8,128)(2,1)S(1)}, bf16[2,2,512,128]{3,2,1,0:T(8,128)(2,1)S(1)}, u32[]{:S(2)}, u32[]{:S(2)}) collective-permute-start(bf16[2,2,512,128]{3,2,1,0:T(8,128)(2,1)S(1)} %shard_map.55), channel_id=1, source_target_pairs={{0,64},{1,193},{2,66},{3,195},{4,68},{5,197},{6,70},{7,199},{8,72}... | collective-permute-start | bytes 1572872 | tf_op jit(solution)/shard_map/ppermute | solution.py:31
  6.4 11.7 %collective-permute-start.2 = (bf16[2,2,512,128]{3,2,1,0:T(8,128)(2,1)S(1)}, bf16[2,2,512,128]{3,2,1,0:T(8,128)(2,1)S(1)}, u32[]{:S(2)}, u32[]{:S(2)}) collective-permute-start(bf16[2,2,512,128]{3,2,1,0:T(8,128)(2,1)S(1)} %shard_map.55), channel_id=1, source_target_pairs={{0,8},{1,57},{2,10},{3,59},{4,12},{5,61},{6,14},{7,63},{8,16},{9,1... | collective-permute-start | bytes 1572872 | tf_op jit(solution)/shard_map/ppermute | solution.py:31
  18.1 8.3 %collective-permute-start.3 = (bf16[2,2,512,128]{3,2,1,0:T(8,128)(2,1)S(1)}, bf16[2,2,512,128]{3,2,1,0:T(8,128)(2,1)S(1)}, u32[]{:S(2)}, u32[]{:S(2)}) collective-permute-start(bf16[2,2,512,128]{3,2,1,0:T(8,128)(2,1)S(1)} %collective-permute-done.1.refs_0_.rest_1_), channel_id=1, source_target_pairs={{0,64},{1,193},{2,66},{3,195},{4,68},{5,197},{6,70},{7,199},{8,72}... | collective-permute-start | bytes 1572872 | tf_op jit(solution)/shard_map/ppermute | solution.py:31
  18.7 9.2 %collective-permute-start.4 = (bf16[2,2,512,128]{3,2,1,0:T(8,128)(2,1)S(1)}, bf16[2,2,512,128]{3,2,1,0:T(8,128)(2,1)S(1)}, u32[]{:S(2)}, u32[]{:S(2)}) collective-permute-start(bf16[2,2,512,128]{3,2,1,0:T(8,128)(2,1)S(1)} %collective-permute-done.2.refs_0_.rest_4_), channel_id=1, source_target_pairs={{0,8},{1,57},{2,10},{3,59},{4,12},{5,61},{6,14},{7,63},{8,16},{9,1... | collective-permute-start | bytes 1572872 | tf_op jit(solution)/shard_map/ppermute | solution.py:31
  21.8 6.1 %collective-permute-start.5 = (bf16[2,2,512,128]{3,2,1,0:T(8,128)(2,1)S(1)}, bf16[2,2,512,128]{3,2,1,0:T(8,128)(2,1)S(1)}, u32[]{:S(2)}, u32[]{:S(2)}) collective-permute-start(bf16[2,2,512,128]{3,2,1,0:T(8,128)(2,1)S(1)} %collective-permute-done.1.refs_0_.rest_1_), channel_id=1, source_target_pairs={{0,1},{1,0},{2,3},{3,2},{4,5},{5,4},{6,7},{7,6},{8,9},{9,8},{10,11... | collective-permute-start | bytes 1572872 | tf_op jit(solution)/shard_map/ppermute | solution.py:40
  21.8 6.1 %collective-permute-start.6 = (bf16[2,2,512,128]{3,2,1,0:T(8,128)(2,1)S(1)}, bf16[2,2,512,128]{3,2,1,0:T(8,128)(2,1)S(1)}, u32[]{:S(2)}, u32[]{:S(2)}) collective-permute-start(bf16[2,2,512,128]{3,2,1,0:T(8,128)(2,1)S(1)} %collective-permute-done.2.refs_0_.rest_4_), channel_id=1, source_target_pairs={{0,1},{1,0},{2,3},{3,2},{4,5},{5,4},{6,7},{7,6},{8,9},{9,8},{10,11... | collective-permute-start | bytes 1572872 | tf_op jit(solution)/shard_map/ppermute | solution.py:40
  27.9 4.3 %collective-permute-start.7 = (bf16[2,2,512,128]{3,2,1,0:T(8,128)(2,1)S(1)}, bf16[2,2,512,128]{3,2,1,0:T(8,128)(2,1)S(1)}, u32[]{:S(2)}, u32[]{:S(2)}) collective-permute-start(bf16[2,2,512,128]{3,2,1,0:T(8,128)(2,1)S(1)} %collective-permute-done.4.refs_2_.rest_6_), channel_id=1, source_target_pairs={{0,1},{1,0},{2,3},{3,2},{4,5},{5,4},{6,7},{7,6},{8,9},{9,8},{10,11... | collective-permute-start | bytes 1572872 | tf_op jit(solution)/shard_map/ppermute | solution.py:40
  32.3 18.4 %collective-permute-start.9 = (bf16[2,4,512,128]{3,2,1,0:T(8,128)(2,1)S(1)}, bf16[2,4,512,128]{3,2,1,0:T(8,128)(2,1)S(1)}, u32[]{:S(2)}, u32[]{:S(2)}) collective-permute-start(bf16[2,4,512,128]{3,2,1,0:T(8,128)(2,1)S(1)} %shard_map.58), channel_id=1, source_target_pairs={{0,64},{1,193},{2,66},{3,195},{4,68},{5,197},{6,70},{7,199},{8,72}... | collective-permute-start | bytes 3145736 | tf_op jit(solution)/shard_map/ppermute | solution.py:31
  33.9 16.8 %collective-permute-start.8 = (bf16[2,3,512,128]{3,2,1,0:T(8,128)(2,1)S(1)}, bf16[2,3,512,128]{3,2,1,0:T(8,128)(2,1)S(1)}, u32[]{:S(2)}, u32[]{:S(2)}) collective-permute-start(bf16[2,3,512,128]{3,2,1,0:T(8,128)(2,1)S(1)} %shard_map.57), channel_id=1, source_target_pairs={{0,8},{1,57},{2,10},{3,59},{4,12},{5,61},{6,14},{7,63},{8,16},{9,1... | collective-permute-start | bytes 2359304 | tf_op jit(solution)/shard_map/ppermute | solution.py:31
  34.5 16.2 %collective-permute-start.10 = (bf16[2,2,512,128]{3,2,1,0:T(8,128)(2,1)S(1)}, bf16[2,2,512,128]{3,2,1,0:T(8,128)(2,1)S(1)}, u32[]{:S(2)}, u32[]{:S(2)}) collective-permute-start(bf16[2,2,512,128]{3,2,1,0:T(8,128)(2,1)S(1)} %collective-permute-done.4.refs_2_.rest_6_), channel_id=1, source_target_pairs={{0,8},{1,57},{2,10},{3,59},{4,12},{5,61},{6,14},{7,63},{8,16},{9,1... | collective-permute-start | bytes 1572872 | tf_op jit(solution)/shard_map/ppermute | solution.py:31
  50.8 11.3 %collective-permute-start.14 = (bf16[2,2,512,128]{3,2,1,0:T(8,128)(2,1)S(1)}, bf16[2,2,512,128]{3,2,1,0:T(8,128)(2,1)S(1)}, u32[]{:S(2)}, u32[]{:S(2)}) collective-permute-start(bf16[2,2,512,128]{3,2,1,0:T(8,128)(2,1)S(1)} %collective-permute-done.10.rest_8_.refs_0_), channel_id=1, source_target_pairs={{0,1},{1,0},{2,3},{3,2},{4,5},{5,4},{6,7},{7,6},{8,9},{9,8},{10,11... | collective-permute-start | bytes 1572872 | tf_op jit(solution)/shard_map/ppermute | solution.py:40
  53.0 5.5 %collective-permute-start.11 = (bf16[2,512,128]{2,1,0:T(8,128)(2,1)S(1)}, bf16[2,512,128]{2,1,0:T(8,128)(2,1)S(1)}, u32[]{:S(2)}, u32[]{:S(2)}) collective-permute-start(bf16[2,512,128]{2,1,0:T(8,128)(2,1)S(1)} %slice_bitcast_fusion.6), channel_id=1, source_target_pairs={{0,8},{1,57},{2,10},{3,59},{4,12},{5,61},{6,14},{7,63},{8,16},{9,1... | collective-permute-start | bytes 786440 | tf_op jit(solution)/shard_map/ppermute | solution.py:31
  53.0 13.9 %collective-permute-start.13 = (bf16[2,3,512,128]{3,2,1,0:T(8,128)(2,1)S(1)}, bf16[2,3,512,128]{3,2,1,0:T(8,128)(2,1)S(1)}, u32[]{:S(2)}, u32[]{:S(2)}) collective-permute-start(bf16[2,3,512,128]{3,2,1,0:T(8,128)(2,1)S(1)} %collective-permute-done.8.rest_11_), channel_id=1, source_target_pairs={{0,8},{1,57},{2,10},{3,59},{4,12},{5,61},{6,14},{7,63},{8,16},{9,1... | collective-permute-start | bytes 2359304 | tf_op jit(solution)/shard_map/ppermute | solution.py:31
  53.2 8.9 %collective-permute-start.12 = (bf16[4,512,128]{2,1,0:T(8,128)(2,1)S(1)}, bf16[4,512,128]{2,1,0:T(8,128)(2,1)S(1)}, u32[]{:S(2)}, u32[]{:S(2)}) collective-permute-start(bf16[4,512,128]{2,1,0:T(8,128)(2,1)S(1)} %get-tuple-element.114), channel_id=1, source_target_pairs={{0,64},{1,193},{2,66},{3,195},{4,68},{5,197},{6,70},{7,199},{8,72}... | collective-permute-start | bytes 1572872 | tf_op jit(solution)/shard_map/ppermute | solution.py:31
  55.0 7.1 %collective-permute-start.15 = (bf16[4,512,128]{2,1,0:T(8,128)(2,1)S(1)}, bf16[4,512,128]{2,1,0:T(8,128)(2,1)S(1)}, u32[]{:S(2)}, u32[]{:S(2)}) collective-permute-start(bf16[4,512,128]{2,1,0:T(8,128)(2,1)S(1)} %get-tuple-element.113), channel_id=1, source_target_pairs={{0,1},{1,0},{2,3},{3,2},{4,5},{5,4},{6,7},{7,6},{8,9},{9,8},{10,11... | collective-permute-start | bytes 1572872 | tf_op jit(solution)/shard_map/ppermute | solution.py:40
  58.6 3.5 %collective-permute-start.16 = (bf16[3,512,128]{2,1,0:T(8,128)(2,1)S(1)}, bf16[3,512,128]{2,1,0:T(8,128)(2,1)S(1)}, u32[]{:S(2)}, u32[]{:S(2)}) collective-permute-start(bf16[3,512,128]{2,1,0:T(8,128)(2,1)S(1)} %slice_bitcast_fusion.5), channel_id=1, source_target_pairs={{0,1},{1,0},{2,3},{3,2},{4,5},{5,4},{6,7},{7,6},{8,9},{9,8},{10,11... | collective-permute-start | bytes 1179656 | tf_op jit(solution)/shard_map/ppermute | solution.py:40
  69.4 11.1 %collective-permute-start.18 = (bf16[2,3,512,128]{3,2,1,0:T(8,128)(2,1)S(1)}, bf16[2,3,512,128]{3,2,1,0:T(8,128)(2,1)S(1)}, u32[]{:S(2)}, u32[]{:S(2)}) collective-permute-start(bf16[2,3,512,128]{3,2,1,0:T(8,128)(2,1)S(1)} %collective-permute-done.13.rest_16_), channel_id=1, source_target_pairs={{0,8},{1,57},{2,10},{3,59},{4,12},{5,61},{6,14},{7,63},{8,16},{9,1... | collective-permute-start | bytes 2359304 | tf_op jit(solution)/shard_map/ppermute | solution.py:31
  70.5 11.2 %collective-permute-start.20 = (bf16[2,3,512,128]{3,2,1,0:T(8,128)(2,1)S(1)}, bf16[2,3,512,128]{3,2,1,0:T(8,128)(2,1)S(1)}, u32[]{:S(2)}, u32[]{:S(2)}) collective-permute-start(bf16[2,3,512,128]{3,2,1,0:T(8,128)(2,1)S(1)} %shard_map.60), channel_id=1, source_target_pairs={{0,64},{1,193},{2,66},{3,195},{4,68},{5,197},{6,70},{7,199},{8,72}... | collective-permute-start | bytes 2359304 | tf_op jit(solution)/shard_map/ppermute | solution.py:31
  82.9 4.0 %collective-permute-start.21 = (bf16[1,448,512]{2,1,0:T(8,128)(2,1)S(1)}, bf16[1,448,512]{2,1,0:T(8,128)(2,1)S(1)}, u32[]{:S(2)}, u32[]{:S(2)}) collective-permute-start(bf16[1,448,512]{2,1,0:T(8,128)(2,1)S(1)} %shard_map.61), channel_id=1, source_target_pairs={{0,1},{1,0},{2,3},{3,2},{4,5},{5,4},{6,7},{7,6},{8,9},{9,8},{10,11... | collective-permute-start | bytes 1376264 | tf_op jit(solution)/shard_map/ppermute | solution.py:40
  90.2 5.7 %collective-permute-start.22 = (bf16[3,448,512]{2,1,0:T(8,128)(2,1)S(1)}, bf16[3,448,512]{2,1,0:T(8,128)(2,1)S(1)}, u32[]{:S(2)}, u32[]{:S(2)}) collective-permute-start(bf16[3,448,512]{2,1,0:T(8,128)(2,1)S(1)} %shard_map.63), channel_id=1, source_target_pairs={{0,1},{1,0},{2,3},{3,2},{4,5},{5,4},{6,7},{7,6},{8,9},{9,8},{10,11... | collective-permute-start | bytes 4128776 | tf_op jit(solution)/shard_map/ppermute | solution.py:40
  90.7 7.0 %collective-permute-start.25 = (bf16[3,512,128]{2,1,0:T(8,128)(2,1)S(1)}, bf16[3,512,128]{2,1,0:T(8,128)(2,1)S(1)}, u32[]{:S(2)}, u32[]{:S(2)}) collective-permute-start(bf16[3,512,128]{2,1,0:T(8,128)(2,1)S(1)} %slice_bitcast_fusion.3), channel_id=1, source_target_pairs={{0,8},{1,57},{2,10},{3,59},{4,12},{5,61},{6,14},{7,63},{8,16},{9,1... | collective-permute-start | bytes 1179656 | tf_op jit(solution)/shard_map/ppermute | solution.py:31
  92.5 7.0 %collective-permute-start.26 = (bf16[3,512,128]{2,1,0:T(8,128)(2,1)S(1)}, bf16[3,512,128]{2,1,0:T(8,128)(2,1)S(1)}, u32[]{:S(2)}, u32[]{:S(2)}) collective-permute-start(bf16[3,512,128]{2,1,0:T(8,128)(2,1)S(1)} %slice_bitcast_fusion.2), channel_id=1, source_target_pairs={{0,64},{1,193},{2,66},{3,195},{4,68},{5,197},{6,70},{7,199},{8,72}... | collective-permute-start | bytes 1179656 | tf_op jit(solution)/shard_map/ppermute | solution.py:31
  93.1 7.0 %collective-permute-start.23 = (bf16[224,512]{1,0:T(8,128)(2,1)S(1)}, bf16[224,512]{1,0:T(8,128)(2,1)S(1)}, u32[]{:S(2)}, u32[]{:S(2)}) collective-permute-start(bf16[224,512]{1,0:T(8,128)(2,1)S(1)} %get-tuple-element.86), channel_id=1, source_target_pairs={{0,2},{1,3},{2,4},{3,5},{4,6},{5,7},{6,0},{7,1},{8,10},{9,11},{10,... | collective-permute-start | bytes 688136 | tf_op jit(solution)/shard_map/ppermute | solution.py:36
  94.4 6.1 %collective-permute-start.24 = (bf16[224,512]{1,0:T(8,128)(2,1)S(1)}, bf16[224,512]{1,0:T(8,128)(2,1)S(1)}, u32[]{:S(2)}, u32[]{:S(2)}) collective-permute-start(bf16[224,512]{1,0:T(8,128)(2,1)S(1)} %get-tuple-element.87), channel_id=1, source_target_pairs={{0,6},{1,7},{2,0},{3,1},{4,2},{5,3},{6,4},{7,5},{8,14},{9,15},{10,... | collective-permute-start | bytes 688136 | tf_op jit(solution)/shard_map/ppermute | solution.py:36
  100.8 12.9 %collective-permute-start.28 = (bf16[448,512]{1,0:T(8,128)(2,1)S(1)}, bf16[448,512]{1,0:T(8,128)(2,1)S(1)}, u32[]{:S(2)}, u32[]{:S(2)}) collective-permute-start(bf16[448,512]{1,0:T(8,128)(2,1)S(1)} %get-tuple-element.99), channel_id=1, source_target_pairs={{0,2},{1,3},{2,4},{3,5},{4,6},{5,7},{6,0},{7,1},{8,10},{9,11},{10,... | collective-permute-start | bytes 1376264 | tf_op jit(solution)/shard_map/ppermute | solution.py:36
  102.1 11.5 %collective-permute-start.29 = (bf16[448,512]{1,0:T(8,128)(2,1)S(1)}, bf16[448,512]{1,0:T(8,128)(2,1)S(1)}, u32[]{:S(2)}, u32[]{:S(2)}) collective-permute-start(bf16[448,512]{1,0:T(8,128)(2,1)S(1)} %get-tuple-element.100), channel_id=1, source_target_pairs={{0,6},{1,7},{2,0},{3,1},{4,2},{5,3},{6,4},{7,5},{8,14},{9,15},{10,... | collective-permute-start | bytes 1376264 | tf_op jit(solution)/shard_map/ppermute | solution.py:36
  120.6 3.8 %collective-permute-start.31 = (bf16[3,576,512]{2,1,0:T(8,128)(2,1)S(1)}, bf16[3,576,512]{2,1,0:T(8,128)(2,1)S(1)}, u32[]{:S(2)}, u32[]{:S(2)}) collective-permute-start(bf16[3,576,512]{2,1,0:T(8,128)(2,1)S(1)} %shard_map.71), channel_id=1, source_target_pairs={{0,1},{1,0},{2,3},{3,2},{4,5},{5,4},{6,7},{7,6},{8,9},{9,8},{10,11... | collective-permute-start | bytes 5308424 | tf_op jit(solution)/shard_map/ppermute | solution.py:40
  121.1 10.0 %collective-permute-start.32 = (bf16[288,512]{1,0:T(8,128)(2,1)S(1)}, bf16[288,512]{1,0:T(8,128)(2,1)S(1)}, u32[]{:S(2)}, u32[]{:S(2)}) collective-permute-start(bf16[288,512]{1,0:T(8,128)(2,1)S(1)} %get-tuple-element.109), channel_id=1, source_target_pairs={{0,2},{1,3},{2,4},{3,5},{4,6},{5,7},{6,0},{7,1},{8,10},{9,11},{10,... | collective-permute-start | bytes 884744 | tf_op jit(solution)/shard_map/ppermute | solution.py:36
  122.1 9.0 %collective-permute-start.33 = (bf16[288,512]{1,0:T(8,128)(2,1)S(1)}, bf16[288,512]{1,0:T(8,128)(2,1)S(1)}, u32[]{:S(2)}, u32[]{:S(2)}) collective-permute-start(bf16[288,512]{1,0:T(8,128)(2,1)S(1)} %get-tuple-element.110), channel_id=1, source_target_pairs={{0,6},{1,7},{2,0},{3,1},{4,2},{5,3},{6,4},{7,5},{8,14},{9,15},{10,... | collective-permute-start | bytes 884744 | tf_op jit(solution)/shard_map/ppermute | solution.py:36
  131.2 15.3 %collective-permute-start.34 = (bf16[576,512]{1,0:T(8,128)(2,1)S(1)}, bf16[576,512]{1,0:T(8,128)(2,1)S(1)}, u32[]{:S(2)}, u32[]{:S(2)}) collective-permute-start(bf16[576,512]{1,0:T(8,128)(2,1)S(1)} %get-tuple-element.111), channel_id=1, source_target_pairs={{0,2},{1,3},{2,4},{3,5},{4,6},{5,7},{6,0},{7,1},{8,10},{9,11},{10,... | collective-permute-start | bytes 1769480 | tf_op jit(solution)/shard_map/ppermute | solution.py:36
  131.7 14.8 %collective-permute-start.35 = (bf16[576,512]{1,0:T(8,128)(2,1)S(1)}, bf16[576,512]{1,0:T(8,128)(2,1)S(1)}, u32[]{:S(2)}, u32[]{:S(2)}) collective-permute-start(bf16[576,512]{1,0:T(8,128)(2,1)S(1)} %get-tuple-element.112), channel_id=1, source_target_pairs={{0,6},{1,7},{2,0},{3,1},{4,2},{5,3},{6,4},{7,5},{8,14},{9,15},{10,... | collective-permute-start | bytes 1769480 | tf_op jit(solution)/shard_map/ppermute | solution.py:36
  (11 other events, 91.1 us)
where the time goes:
time: 150 us; the launch traced here: 149 us
  waiting for transfers between devices  62 us (41%)
  starting transfers between devices  48.8 us (33%)
  Pallas kernels  35.7 us (24%)
  local copies, waits for them, and re-layouts  1.84 us (1%)
    ppermute x14, waiting for transfers between devices, send_cache(): return lax.ppermute(value, ('cache', 'tensor'), pairs)  35.1 us
    ppermute x14, starting transfers between devices, send_cache(): return lax.ppermute(value, ('cache', 'tensor'), pairs)  19.1 us
    ppermute x14, starting transfers between devices, swap_core(): return lax.ppermute(value, 'tensor', [(t, t ^ 1) for t in range(2 * NY)])  18.5 us
    ppermute x8, waiting for transfers between devices, send_y(): return lax.ppermute(value, 'tensor', pairs)  16.3 us
    pallas_call x10, Pallas kernels, project(): pl.pallas_call(kernel, out_shape=out_shape, in_specs=[pl.BlockSpec(memory...  15.9 us
    pallas_call x2, Pallas kernels, attend(): pl.pallas_call(functools.partial(attention_kernel, places, len(arrays), l...  14.3 us
    ppermute x8, starting transfers between devices, send_y(): return lax.ppermute(value, 'tensor', pairs)  11.3 us
    ppermute x14, waiting for transfers between devices, swap_core(): return lax.ppermute(value, 'tensor', [(t, t ^ 1) for t in range(2 * NY)])  10.5 us
  transfers between devices with their start and end apart: 36, of which 22 were waited for; matrix products, arithmetic and copies ran while one was open for 0% of the time, Pallas kernels for 17%

commit v1 on v0

--- a/solution.py
+++ b/solution.py
@@ -416,8 +416,8 @@
         near, *self.tokens = together(near, *tokens)
         self.near = swap_core(near)
         self.project = functools.partial(project_own, place, mine, w_out)
-        top2, low2 = self.project((2,), self.near, 0, True)
-        later, self.top2, self.low2 = together(mine, top2, low2)
+        self.top2, self.low2 = self.project((2,), self.near, 0, True)
+        later, _ = together(mine, near)
         self.rest = swap_core(project_other(place, later, w_out, (1, 3, 0), width))
 
     def across(self):
@@ -443,7 +443,8 @@
 
     mine = attend(order, codes, queries, suffix_kv, sources, 0, chunk, length)
     gather.late()
-    mine = gather.last(mine.reshape(chunk * suffix, width))
+    mine = mine.reshape(chunk * suffix, width)
+    gather.last(mine)
     one = Projection(info, w_out, mine, out_width)
     top2, low2 = one.across()
     up, down = one.beside()

time: 150 us -> 148 us (0.987)
    ppermute x8, waiting for transfers between devices: 16.3 us -> 20 us  [send_y(): return lax.ppermute(value, 'tensor', pairs)]
    ppermute x14, waiting for transfers between devices: 35.1 us -> 32.1 us  [send_cache(): return lax.ppermute(value, ('cache', 'tensor'), pairs)]
    ppermute x14, starting transfers between devices: 18.5 us -> 16 us  [swap_core(): return lax.ppermute(value, 'tensor', [(t, t ^ 1) for t in range(2 * NY)])]
  transfers between devices with their start and end apart: 36 -> 36, of which waited for: 22 -> 16; matrix products, arithmetic and copies ran while one was open for 0% -> 0% of each run, Pallas kernels for 17% -> 21%
where the time goes in v1:
time: 148 us; the launch traced here: 147 us
  waiting for transfers between devices  61.9 us (42%)
  starting transfers between devices  47.7 us (32%)
  Pallas kernels  35.7 us (24%)
  local copies, waits for them, and re-layouts  1.84 us (1%)
    ppermute x14, waiting for transfers between devices, send_cache(): return lax.ppermute(value, ('cache', 'tensor'), pairs)  32.1 us
    ppermute x8, waiting for transfers between devices, send_y(): return lax.ppermute(value, 'tensor', pairs)  20 us
    ppermute x14, starting transfers between devices, send_cache(): return lax.ppermute(value, ('cache', 'tensor'), pairs)  19.8 us
    ppermute x14, starting transfers between devices, swap_core(): return lax.ppermute(value, 'tensor', [(t, t ^ 1) for t in range(2 * NY)])  16 us
    pallas_call x10, Pallas kernels, project(): pl.pallas_call(kernel, out_shape=out_shape, in_specs=[pl.BlockSpec(memory...  15.9 us
    pallas_call x2, Pallas kernels, attend(): pl.pallas_call(functools.partial(attention_kernel, places, len(arrays), l...  14.3 us
    ppermute x8, starting transfers between devices, send_y(): return lax.ppermute(value, 'tensor', pairs)  11.9 us
    ppermute x14, waiting for transfers between devices, swap_core(): return lax.ppermute(value, 'tensor', [(t, t ^ 1) for t in range(2 * NY)])  9.85 us
  transfers between devices with their start and end apart: 36, of which 16 were waited for; matrix products, arithmetic and copies ran while one was open for 0% of the time, Pallas kernels for 21%

profile of v1, /device:TPU:1, one launch (start us, length us, event | category | flops | bytes accessed | tf_op | source)
XLA Modules:
  0.0 147.4 jit_solution(14214834398319623703)
XLA Ops:
  0.0 3.2 %collective-permute-start = (bf16[2,512,128]{2,1,0:T(8,128)(2,1)}, bf16[2,512,128]{2,1,0:T(8,128)(2,1)S(1)}, u32[]{:S(2)}, u32[]{:S(2)}) collective-permute-start(bf16[2,512,128]{2,1,0:T(8,128)(2,1)} %bitcast.30), channel_id=1, source_target_pairs={{0,1},{1,0},{2,3},{3,2},{4,5},{5,4},{6,7},{7,6},{8,9},{9,8},{10,11... | collective-permute-start | bytes 786440 | tf_op jit(solution)/shard_map/ppermute | solution.py:40
  6.4 5.6 %collective-permute-start.2 = (bf16[2,2,512,128]{3,2,1,0:T(8,128)(2,1)S(1)}, bf16[2,2,512,128]{3,2,1,0:T(8,128)(2,1)S(1)}, u32[]{:S(2)}, u32[]{:S(2)}) collective-permute-start(bf16[2,2,512,128]{3,2,1,0:T(8,128)(2,1)S(1)} %shard_map.55), channel_id=1, source_target_pairs={{0,8},{1,57},{2,10},{3,59},{4,12},{5,61},{6,14},{7,63},{8,16},{9,1... | collective-permute-start | bytes 1572872 | tf_op jit(solution)/shard_map/ppermute | solution.py:31
  12.7 2.9 %shard_map.56 = (s32[32]{0:T(128)S(1)}, s32[32]{0:T(128)S(1)}, s32[2]{0:T(128)S(1)}) custom-call(s32[32]{0:T(128)S(1)} %bitcast.34), custom_call_target="tpu_custom_call" | custom-call | flops 1000 | bytes 1000 | tf_op jit(solution)/shard_map/pallas_call | solution.py:220
  15.6 2.5 %collective-permute-done.2.refs_0_.rest_4_ = bf16[2,2,512,128]{3,2,1,0:T(8,128)(2,1)S(1)} collective-permute-done((bf16[2,2,512,128]{3,2,1,0:T(8,128)(2,1)S(1)}, bf16[2,2,512,128]{3,2,1,0:T(8,128)(2,1)S(1)}, u32[]{:S(2)}, u32[]{:S(2)}) %collective-permute-start.2) | collective-permute-done | bytes 524320 | tf_op jit(solution)/shard_map/ppermute | solution.py:31
  18.7 3.1 %collective-permute-start.4 = (bf16[2,2,512,128]{3,2,1,0:T(8,128)(2,1)S(1)}, bf16[2,2,512,128]{3,2,1,0:T(8,128)(2,1)S(1)}, u32[]{:S(2)}, u32[]{:S(2)}) collective-permute-start(bf16[2,2,512,128]{3,2,1,0:T(8,128)(2,1)S(1)} %collective-permute-done.2.refs_0_.rest_4_), channel_id=1, source_target_pairs={{0,8},{1,57},{2,10},{3,59},{4,12},{5,61},{6,14},{7,63},{8,16},{9,1... | collective-permute-start | bytes 1572872 | tf_op jit(solution)/shard_map/ppermute | solution.py:31
  22.3 4.2 %collective-permute-done.3.refs_2_.rest_3_ = bf16[2,2,512,128]{3,2,1,0:T(8,128)(2,1)S(1)} collective-permute-done((bf16[2,2,512,128]{3,2,1,0:T(8,128)(2,1)S(1)}, bf16[2,2,512,128]{3,2,1,0:T(8,128)(2,1)S(1)}, u32[]{:S(2)}, u32[]{:S(2)}) %collective-permute-start.3) | collective-permute-done | bytes 524320 | tf_op jit(solution)/shard_map/ppermute | solution.py:31
  27.9 2.8 %collective-permute-start.7 = (bf16[2,2,512,128]{3,2,1,0:T(8,128)(2,1)S(1)}, bf16[2,2,512,128]{3,2,1,0:T(8,128)(2,1)S(1)}, u32[]{:S(2)}, u32[]{:S(2)}) collective-permute-start(bf16[2,2,512,128]{3,2,1,0:T(8,128)(2,1)S(1)} %collective-permute-done.4.refs_2_.rest_6_), channel_id=1, source_target_pairs={{0,1},{1,0},{2,3},{3,2},{4,5},{5,4},{6,7},{7,6},{8,9},{9,8},{10,11... | collective-permute-start | bytes 1572872 | tf_op jit(solution)/shard_map/ppermute | solution.py:40
  30.7 1.5 %collective-permute-done.7.refs_3_.rest_7_ = bf16[2,2,512,128]{3,2,1,0:T(8,128)(2,1)S(1)} collective-permute-done((bf16[2,2,512,128]{3,2,1,0:T(8,128)(2,1)S(1)}, bf16[2,2,512,128]{3,2,1,0:T(8,128)(2,1)S(1)}, u32[]{:S(2)}, u32[]{:S(2)}) %collective-permute-start.7) | collective-permute-done | bytes 524320 | tf_op jit(solution)/shard_map/ppermute | solution.py:40
  32.3 1.5 %collective-permute-start.9 = (bf16[2,4,512,128]{3,2,1,0:T(8,128)(2,1)S(1)}, bf16[2,4,512,128]{3,2,1,0:T(8,128)(2,1)S(1)}, u32[]{:S(2)}, u32[]{:S(2)}) collective-permute-start(bf16[2,4,512,128]{3,2,1,0:T(8,128)(2,1)S(1)} %shard_map.58), channel_id=1, source_target_pairs={{0,64},{1,193},{2,66},{3,195},{4,68},{5,197},{6,70},{7,199},{8,72}... | collective-permute-start | bytes 3145736 | tf_op jit(solution)/shard_map/ppermute | solution.py:31
  35.3 15.5 %collective-permute-done.10.rest_8_.refs_0_ = bf16[2,2,512,128]{3,2,1,0:T(8,128)(2,1)S(1)} collective-permute-done((bf16[2,2,512,128]{3,2,1,0:T(8,128)(2,1)S(1)}, bf16[2,2,512,128]{3,2,1,0:T(8,128)(2,1)S(1)}, u32[]{:S(2)}, u32[]{:S(2)}) %collective-permute-start.10) | collective-permute-done | bytes 524320 | tf_op jit(solution)/shard_map/ppermute | solution.py:31
  50.8 2.3 %collective-permute-start.14 = (bf16[2,2,512,128]{3,2,1,0:T(8,128)(2,1)S(1)}, bf16[2,2,512,128]{3,2,1,0:T(8,128)(2,1)S(1)}, u32[]{:S(2)}, u32[]{:S(2)}) collective-permute-start(bf16[2,2,512,128]{3,2,1,0:T(8,128)(2,1)S(1)} %collective-permute-done.10.rest_8_.refs_0_), channel_id=1, source_target_pairs={{0,1},{1,0},{2,3},{3,2},{4,5},{5,4},{6,7},{7,6},{8,9},{9,8},{10,11... | collective-permute-start | bytes 1572872 | tf_op jit(solution)/shard_map/ppermute | solution.py:40
  53.2 1.8 %collective-permute-start.12 = (bf16[4,512,128]{2,1,0:T(8,128)(2,1)S(1)}, bf16[4,512,128]{2,1,0:T(8,128)(2,1)S(1)}, u32[]{:S(2)}, u32[]{:S(2)}) collective-permute-start(bf16[4,512,128]{2,1,0:T(8,128)(2,1)S(1)} %get-tuple-element.104), channel_id=1, source_target_pairs={{0,64},{1,193},{2,66},{3,195},{4,68},{5,197},{6,70},{7,199},{8,72}... | collective-permute-start | bytes 1572872 | tf_op jit(solution)/shard_map/ppermute | solution.py:31
  55.1 3.5 %collective-permute-done.11.rest_10_.refs_2_ = bf16[2,512,128]{2,1,0:T(8,128)(2,1)S(1)} collective-permute-done((bf16[2,512,128]{2,1,0:T(8,128)(2,1)S(1)}, bf16[2,512,128]{2,1,0:T(8,128)(2,1)S(1)}, u32[]{:S(2)}, u32[]{:S(2)}) %collective-permute-start.11) | collective-permute-done | bytes 262176 | tf_op jit(solution)/shard_map/ppermute | solution.py:31
  58.6 2.2 %collective-permute-start.16 = (bf16[3,512,128]{2,1,0:T(8,128)(2,1)S(1)}, bf16[3,512,128]{2,1,0:T(8,128)(2,1)S(1)}, u32[]{:S(2)}, u32[]{:S(2)}) collective-permute-start(bf16[3,512,128]{2,1,0:T(8,128)(2,1)S(1)} %slice_bitcast_fusion.5), channel_id=1, source_target_pairs={{0,1},{1,0},{2,3},{3,2},{4,5},{5,4},{6,7},{7,6},{8,9},{9,8},{10,11... | collective-permute-start | bytes 1179656 | tf_op jit(solution)/shard_map/ppermute | solution.py:40
  62.1 4.9 %collective-permute-done.13.rest_16_ = bf16[2,3,512,128]{3,2,1,0:T(8,128)(2,1)S(1)} collective-permute-done((bf16[2,3,512,128]{3,2,1,0:T(8,128)(2,1)S(1)}, bf16[2,3,512,128]{3,2,1,0:T(8,128)(2,1)S(1)}, u32[]{:S(2)}, u32[]{:S(2)}) %collective-permute-start.13) | collective-permute-done | bytes 786464 | tf_op jit(solution)/shard_map/ppermute | solution.py:31
  67.0 2.4 %collective-permute-start.17 = (bf16[3,512,128]{2,1,0:T(8,128)(2,1)S(1)}, bf16[3,512,128]{2,1,0:T(8,128)(2,1)S(1)}, u32[]{:S(2)}, u32[]{:S(2)}) collective-permute-start(bf16[3,512,128]{2,1,0:T(8,128)(2,1)S(1)} %slice_bitcast_fusion.4), channel_id=1, source_target_pairs={{0,1},{1,0},{2,3},{3,2},{4,5},{5,4},{6,7},{7,6},{8,9},{9,8},{10,11... | collective-permute-start | bytes 1179656 | tf_op jit(solution)/shard_map/ppermute | solution.py:40
  71.1 1.8 %collective-permute-start.24 = (bf16[2,3,512,128]{3,2,1,0:T(8,128)(2,1)S(1)}, bf16[2,3,512,128]{3,2,1,0:T(8,128)(2,1)S(1)}, u32[]{:S(2)}, u32[]{:S(2)}) collective-permute-start(bf16[2,3,512,128]{3,2,1,0:T(8,128)(2,1)S(1)} %shard_map.65), channel_id=1, source_target_pairs={{0,64},{1,193},{2,66},{3,195},{4,68},{5,197},{6,70},{7,199},{8,72}... | collective-permute-start | bytes 2359304 | tf_op jit(solution)/shard_map/ppermute | solution.py:31
  72.9 6.3 %shard_map.59 = bf16[14,32,1024]{2,1,0:T(8,128)(2,1)S(1)} custom-call(s32[32]{0:T(128)S(1)} %get-tuple-element.82.order, s32[32]{0:T(128)S(1)} %get-tuple-element.59.codes, bf16[32,32,1024]{2,1,0:T(8,128)(2,1)S(1)} %copy-done, bf16[2,32,32,128]{3,2,1,0:T(8,128)(2,1)S(1)} %copy-done.3, bf16[2,512,128]{2,1,0:T(8,128)(2,1)S(1)} %bitcast.32, ...), custom_call_target="tpu_custom_call" | custom-call | flops 939524096 | bytes 8388608 | tf_op jit(solution)/shard_map/pallas_call | solution.py:306
  80.5 2.1 %shard_map.61 = bf16[3,448,512]{2,1,0:T(8,128)(2,1)S(1)} custom-call(s32[2]{0:T(128)S(1)} %get-tuple-element.58.place, bf16[448,1024]{1,0:T(8,128)(2,1)S(1)} %bitcast.26, bf16[1024,4096]{1,0:T(8,128)(2,1)S(1)} %bitcast.19), custom_call_target="tpu_custom_call" | custom-call | flops 1409286144 | bytes 4194304 | tf_op jit(solution)/shard_map/pallas_call | solution.py:357
  83.7 2.6 %collective-permute-start.26 = (bf16[3,512,128]{2,1,0:T(8,128)(2,1)S(1)}, bf16[3,512,128]{2,1,0:T(8,128)(2,1)S(1)}, u32[]{:S(2)}, u32[]{:S(2)}) collective-permute-start(bf16[3,512,128]{2,1,0:T(8,128)(2,1)S(1)} %slice_bitcast_fusion.2), channel_id=1, source_target_pairs={{0,64},{1,193},{2,66},{3,195},{4,68},{5,197},{6,70},{7,199},{8,72}... | collective-permute-start | bytes 1179656 | tf_op jit(solution)/shard_map/ppermute | solution.py:31
  90.6 1.7 %shard_map.63 = (bf16[448,512]{1,0:T(8,128)(2,1)S(1)}, bf16[448,512]{1,0:T(8,128)(2,1)S(1)}) custom-call(s32[2]{0:T(128)S(1)} %get-tuple-element.58.place, bf16[448,1024]{1,0:T(8,128)(2,1)S(1)} %bitcast.28, bf16[1024,4096]{1,0:T(8,128)(2,1)S(1)} %bitcast.19, bf16[3,448,512]{2,1,0:T(8,128)(2,1)S(1)} %collective-permute-done.18.came_ref), custom_call_target="tpu_custom_call" | custom-call | flops 939524096 | bytes 4194304 | tf_op jit(solution)/shard_map/pallas_call | solution.py:357
  92.3 3.9 %collective-permute-done.20.top = bf16[224,512]{1,0:T(8,128)(2,1)S(1)} collective-permute-done((bf16[224,512]{1,0:T(8,128)(2,1)S(1)}, bf16[224,512]{1,0:T(8,128)(2,1)S(1)}, u32[]{:S(2)}, u32[]{:S(2)}) %collective-permute-start.20) | collective-permute-done | bytes 229408 | tf_op jit(solution)/shard_map/ppermute | solution.py:36
  98.7 1.8 %collective-permute-start.29 = (bf16[448,512]{1,0:T(8,128)(2,1)S(1)}, bf16[448,512]{1,0:T(8,128)(2,1)S(1)}, u32[]{:S(2)}, u32[]{:S(2)}) collective-permute-start(bf16[448,512]{1,0:T(8,128)(2,1)S(1)} %get-tuple-element.92), channel_id=1, source_target_pairs={{0,6},{1,7},{2,0},{3,1},{4,2},{5,3},{6,4},{7,5},{8,14},{9,15},{10,... | collective-permute-start | bytes 1376264 | tf_op jit(solution)/shard_map/ppermute | solution.py:36
  100.5 8.0 %shard_map.67 = bf16[18,32,1024]{2,1,0:T(8,128)(2,1)S(1)} custom-call(s32[32]{0:T(128)S(1)} %get-tuple-element.82.order, s32[32]{0:T(128)S(1)} %get-tuple-element.59.codes, bf16[32,32,1024]{2,1,0:T(8,128)(2,1)S(1)} %copy-done, bf16[2,32,32,128]{3,2,1,0:T(8,128)(2,1)S(1)} %copy-done.3, bf16[2,512,128]{2,1,0:T(8,128)(2,1)S(1)} %bitcast.33, ...), custom_call_target="tpu_custom_call" | custom-call | flops 1207959552 | bytes 8388608 | tf_op jit(solution)/shard_map/pallas_call | solution.py:306
  110.9 2.5 %shard_map.70 = bf16[3,576,512]{2,1,0:T(8,128)(2,1)S(1)} custom-call(s32[2]{0:T(128)S(1)} %get-tuple-element.58.place, bf16[576,1024]{1,0:T(8,128)(2,1)S(1)} %bitcast.21, bf16[1024,4096]{1,0:T(8,128)(2,1)S(1)} %bitcast.19), custom_call_target="tpu_custom_call" | custom-call | flops 1811939328 | bytes 4194304 | tf_op jit(solution)/shard_map/pallas_call | solution.py:357
  114.4 4.1 %collective-permute-done.31.came_ref = bf16[1,576,512]{2,1,0:T(8,128)(2,1)S(1)} collective-permute-done((bf16[1,576,512]{2,1,0:T(8,128)(2,1)S(1)}, bf16[1,576,512]{2,1,0:T(8,128)(2,1)S(1)}, u32[]{:S(2)}, u32[]{:S(2)}) %collective-permute-start.31) | collective-permute-done | bytes 589856 | tf_op jit(solution)/shard_map/ppermute | solution.py:40
  120.9 2.1 %collective-permute-start.33 = (bf16[288,512]{1,0:T(8,128)(2,1)S(1)}, bf16[288,512]{1,0:T(8,128)(2,1)S(1)}, u32[]{:S(2)}, u32[]{:S(2)}) collective-permute-start(bf16[288,512]{1,0:T(8,128)(2,1)S(1)} %get-tuple-element.100), channel_id=1, source_target_pairs={{0,6},{1,7},{2,0},{3,1},{4,2},{5,3},{6,4},{7,5},{8,14},{9,15},{10,... | collective-permute-start | bytes 884744 | tf_op jit(solution)/shard_map/ppermute | solution.py:36
  122.9 1.9 %shard_map.72 = (bf16[576,512]{1,0:T(8,128)(2,1)S(1)}, bf16[576,512]{1,0:T(8,128)(2,1)S(1)}) custom-call(s32[2]{0:T(128)S(1)} %get-tuple-element.58.place, bf16[576,1024]{1,0:T(8,128)(2,1)S(1)} %bitcast.23, bf16[1024,4096]{1,0:T(8,128)(2,1)S(1)} %bitcast.19, bf16[3,576,512]{2,1,0:T(8,128)(2,1)S(1)} %collective-permute-done.30.came_ref), custom_call_target="tpu_custom_call" | custom-call | flops 1207959552 | bytes 4194304 | tf_op jit(solution)/shard_map/pallas_call | solution.py:357
  124.9 5.0 %collective-permute-done.32.top = bf16[288,512]{1,0:T(8,128)(2,1)S(1)} collective-permute-done((bf16[288,512]{1,0:T(8,128)(2,1)S(1)}, bf16[288,512]{1,0:T(8,128)(2,1)S(1)}, u32[]{:S(2)}, u32[]{:S(2)}) %collective-permute-start.32) | collective-permute-done | bytes 294944 | tf_op jit(solution)/shard_map/ppermute | solution.py:36
  130.5 2.4 %collective-permute-start.35 = (bf16[576,512]{1,0:T(8,128)(2,1)S(1)}, bf16[576,512]{1,0:T(8,128)(2,1)S(1)}, u32[]{:S(2)}, u32[]{:S(2)}) collective-permute-start(bf16[576,512]{1,0:T(8,128)(2,1)S(1)} %get-tuple-element.102), channel_id=1, source_target_pairs={{0,6},{1,7},{2,0},{3,1},{4,2},{5,3},{6,4},{7,5},{8,14},{9,15},{10,... | collective-permute-start | bytes 1769480 | tf_op jit(solution)/shard_map/ppermute | solution.py:36
  135.4 10.0 %collective-permute-done.34.refs_4_ = bf16[576,512]{1,0:T(8,128)(2,1)S(1)} collective-permute-done((bf16[576,512]{1,0:T(8,128)(2,1)S(1)}, bf16[576,512]{1,0:T(8,128)(2,1)S(1)}, u32[]{:S(2)}, u32[]{:S(2)}) %collective-permute-start.34) | collective-permute-done | bytes 589856 | tf_op jit(solution)/shard_map/ppermute | solution.py:36
  145.3 2.1 %shard_map.75 = bf16[32,32,512]{2,1,0:T(8,128)(2,1)} custom-call(s32[32]{0:T(128)S(1)} %get-tuple-element.82.order, bf16[448,512]{1,0:T(8,128)(2,1)S(1)} %shard_map.62.refs_0_, bf16[448,512]{1,0:T(8,128)(2,1)S(1)} %collective-permute-done.28.refs_1_, bf16[448,512]{1,0:T(8,128)(2,1)S(1)} %collective-permute-done.29.refs_2_, ...), custom_call_target="tpu_custom_call" | custom-call | tf_op jit(solution)/shard_map/pallas_call | solution.py:463
  (83 shorter events, 28.9 us)
Async XLA Ops:
  0.0 4.6 %collective-permute-start = (bf16[2,512,128]{2,1,0:T(8,128)(2,1)}, bf16[2,512,128]{2,1,0:T(8,128)(2,1)S(1)}, u32[]{:S(2)}, u32[]{:S(2)}) collective-permute-start(bf16[2,512,128]{2,1,0:T(8,128)(2,1)} %bitcast.30), channel_id=1, source_target_pairs={{0,1},{1,0},{2,3},{3,2},{4,5},{5,4},{6,7},{7,6},{8,9},{9,8},{10,11... | collective-permute-start | bytes 786440 | tf_op jit(solution)/shard_map/ppermute | solution.py:40
  5.6 10.0 %collective-permute-start.1 = (bf16[2,2,512,128]{3,2,1,0:T(8,128)(2,1)S(1)}, bf16[2,2,512,128]{3,2,1,0:T(8,128)(2,1)S(1)}, u32[]{:S(2)}, u32[]{:S(2)}) collective-permute-start(bf16[2,2,512,128]{3,2,1,0:T(8,128)(2,1)S(1)} %shard_map.55), channel_id=1, source_target_pairs={{0,64},{1,193},{2,66},{3,195},{4,68},{5,197},{6,70},{7,199},{8,72}... | collective-permute-start | bytes 1572872 | tf_op jit(solution)/shard_map/ppermute | solution.py:31
  6.4 11.7 %collective-permute-start.2 = (bf16[2,2,512,128]{3,2,1,0:T(8,128)(2,1)S(1)}, bf16[2,2,512,128]{3,2,1,0:T(8,128)(2,1)S(1)}, u32[]{:S(2)}, u32[]{:S(2)}) collective-permute-start(bf16[2,2,512,128]{3,2,1,0:T(8,128)(2,1)S(1)} %shard_map.55), channel_id=1, source_target_pairs={{0,8},{1,57},{2,10},{3,59},{4,12},{5,61},{6,14},{7,63},{8,16},{9,1... | collective-permute-start | bytes 1572872 | tf_op jit(solution)/shard_map/ppermute | solution.py:31
  18.1 8.3 %collective-permute-start.3 = (bf16[2,2,512,128]{3,2,1,0:T(8,128)(2,1)S(1)}, bf16[2,2,512,128]{3,2,1,0:T(8,128)(2,1)S(1)}, u32[]{:S(2)}, u32[]{:S(2)}) collective-permute-start(bf16[2,2,512,128]{3,2,1,0:T(8,128)(2,1)S(1)} %collective-permute-done.1.refs_0_.rest_1_), channel_id=1, source_target_pairs={{0,64},{1,193},{2,66},{3,195},{4,68},{5,197},{6,70},{7,199},{8,72}... | collective-permute-start | bytes 1572872 | tf_op jit(solution)/shard_map/ppermute | solution.py:31
  18.7 9.2 %collective-permute-start.4 = (bf16[2,2,512,128]{3,2,1,0:T(8,128)(2,1)S(1)}, bf16[2,2,512,128]{3,2,1,0:T(8,128)(2,1)S(1)}, u32[]{:S(2)}, u32[]{:S(2)}) collective-permute-start(bf16[2,2,512,128]{3,2,1,0:T(8,128)(2,1)S(1)} %collective-permute-done.2.refs_0_.rest_4_), channel_id=1, source_target_pairs={{0,8},{1,57},{2,10},{3,59},{4,12},{5,61},{6,14},{7,63},{8,16},{9,1... | collective-permute-start | bytes 1572872 | tf_op jit(solution)/shard_map/ppermute | solution.py:31
  21.8 6.1 %collective-permute-start.5 = (bf16[2,2,512,128]{3,2,1,0:T(8,128)(2,1)S(1)}, bf16[2,2,512,128]{3,2,1,0:T(8,128)(2,1)S(1)}, u32[]{:S(2)}, u32[]{:S(2)}) collective-permute-start(bf16[2,2,512,128]{3,2,1,0:T(8,128)(2,1)S(1)} %collective-permute-done.1.refs_0_.rest_1_), channel_id=1, source_target_pairs={{0,1},{1,0},{2,3},{3,2},{4,5},{5,4},{6,7},{7,6},{8,9},{9,8},{10,11... | collective-permute-start | bytes 1572872 | tf_op jit(solution)/shard_map/ppermute | solution.py:40
  21.8 6.1 %collective-permute-start.6 = (bf16[2,2,512,128]{3,2,1,0:T(8,128)(2,1)S(1)}, bf16[2,2,512,128]{3,2,1,0:T(8,128)(2,1)S(1)}, u32[]{:S(2)}, u32[]{:S(2)}) collective-permute-start(bf16[2,2,512,128]{3,2,1,0:T(8,128)(2,1)S(1)} %collective-permute-done.2.refs_0_.rest_4_), channel_id=1, source_target_pairs={{0,1},{1,0},{2,3},{3,2},{4,5},{5,4},{6,7},{7,6},{8,9},{9,8},{10,11... | collective-permute-start | bytes 1572872 | tf_op jit(solution)/shard_map/ppermute | solution.py:40
  27.9 4.3 %collective-permute-start.7 = (bf16[2,2,512,128]{3,2,1,0:T(8,128)(2,1)S(1)}, bf16[2,2,512,128]{3,2,1,0:T(8,128)(2,1)S(1)}, u32[]{:S(2)}, u32[]{:S(2)}) collective-permute-start(bf16[2,2,512,128]{3,2,1,0:T(8,128)(2,1)S(1)} %collective-permute-done.4.refs_2_.rest_6_), channel_id=1, source_target_pairs={{0,1},{1,0},{2,3},{3,2},{4,5},{5,4},{6,7},{7,6},{8,9},{9,8},{10,11... | collective-permute-start | bytes 1572872 | tf_op jit(solution)/shard_map/ppermute | solution.py:40
  32.3 18.4 %collective-permute-start.9 = (bf16[2,4,512,128]{3,2,1,0:T(8,128)(2,1)S(1)}, bf16[2,4,512,128]{3,2,1,0:T(8,128)(2,1)S(1)}, u32[]{:S(2)}, u32[]{:S(2)}) collective-permute-start(bf16[2,4,512,128]{3,2,1,0:T(8,128)(2,1)S(1)} %shard_map.58), channel_id=1, source_target_pairs={{0,64},{1,193},{2,66},{3,195},{4,68},{5,197},{6,70},{7,199},{8,72}... | collective-permute-start | bytes 3145736 | tf_op jit(solution)/shard_map/ppermute | solution.py:31
  33.9 16.8 %collective-permute-start.8 = (bf16[2,3,512,128]{3,2,1,0:T(8,128)(2,1)S(1)}, bf16[2,3,512,128]{3,2,1,0:T(8,128)(2,1)S(1)}, u32[]{:S(2)}, u32[]{:S(2)}) collective-permute-start(bf16[2,3,512,128]{3,2,1,0:T(8,128)(2,1)S(1)} %shard_map.57), channel_id=1, source_target_pairs={{0,8},{1,57},{2,10},{3,59},{4,12},{5,61},{6,14},{7,63},{8,16},{9,1... | collective-permute-start | bytes 2359304 | tf_op jit(solution)/shard_map/ppermute | solution.py:31
  34.5 16.2 %collective-permute-start.10 = (bf16[2,2,512,128]{3,2,1,0:T(8,128)(2,1)S(1)}, bf16[2,2,512,128]{3,2,1,0:T(8,128)(2,1)S(1)}, u32[]{:S(2)}, u32[]{:S(2)}) collective-permute-start(bf16[2,2,512,128]{3,2,1,0:T(8,128)(2,1)S(1)} %collective-permute-done.4.refs_2_.rest_6_), channel_id=1, source_target_pairs={{0,8},{1,57},{2,10},{3,59},{4,12},{5,61},{6,14},{7,63},{8,16},{9,1... | collective-permute-start | bytes 1572872 | tf_op jit(solution)/shard_map/ppermute | solution.py:31
  50.8 11.3 %collective-permute-start.14 = (bf16[2,2,512,128]{3,2,1,0:T(8,128)(2,1)S(1)}, bf16[2,2,512,128]{3,2,1,0:T(8,128)(2,1)S(1)}, u32[]{:S(2)}, u32[]{:S(2)}) collective-permute-start(bf16[2,2,512,128]{3,2,1,0:T(8,128)(2,1)S(1)} %collective-permute-done.10.rest_8_.refs_0_), channel_id=1, source_target_pairs={{0,1},{1,0},{2,3},{3,2},{4,5},{5,4},{6,7},{7,6},{8,9},{9,8},{10,11... | collective-permute-start | bytes 1572872 | tf_op jit(solution)/shard_map/ppermute | solution.py:40
  53.0 5.5 %collective-permute-start.11 = (bf16[2,512,128]{2,1,0:T(8,128)(2,1)S(1)}, bf16[2,512,128]{2,1,0:T(8,128)(2,1)S(1)}, u32[]{:S(2)}, u32[]{:S(2)}) collective-permute-start(bf16[2,512,128]{2,1,0:T(8,128)(2,1)S(1)} %slice_bitcast_fusion.6), channel_id=1, source_target_pairs={{0,8},{1,57},{2,10},{3,59},{4,12},{5,61},{6,14},{7,63},{8,16},{9,1... | collective-permute-start | bytes 786440 | tf_op jit(solution)/shard_map/ppermute | solution.py:31
  53.0 13.9 %collective-permute-start.13 = (bf16[2,3,512,128]{3,2,1,0:T(8,128)(2,1)S(1)}, bf16[2,3,512,128]{3,2,1,0:T(8,128)(2,1)S(1)}, u32[]{:S(2)}, u32[]{:S(2)}) collective-permute-start(bf16[2,3,512,128]{3,2,1,0:T(8,128)(2,1)S(1)} %collective-permute-done.8.rest_11_), channel_id=1, source_target_pairs={{0,8},{1,57},{2,10},{3,59},{4,12},{5,61},{6,14},{7,63},{8,16},{9,1... | collective-permute-start | bytes 2359304 | tf_op jit(solution)/shard_map/ppermute | solution.py:31
  53.2 8.9 %collective-permute-start.12 = (bf16[4,512,128]{2,1,0:T(8,128)(2,1)S(1)}, bf16[4,512,128]{2,1,0:T(8,128)(2,1)S(1)}, u32[]{:S(2)}, u32[]{:S(2)}) collective-permute-start(bf16[4,512,128]{2,1,0:T(8,128)(2,1)S(1)} %get-tuple-element.104), channel_id=1, source_target_pairs={{0,64},{1,193},{2,66},{3,195},{4,68},{5,197},{6,70},{7,199},{8,72}... | collective-permute-start | bytes 1572872 | tf_op jit(solution)/shard_map/ppermute | solution.py:31
  55.0 7.1 %collective-permute-start.15 = (bf16[4,512,128]{2,1,0:T(8,128)(2,1)S(1)}, bf16[4,512,128]{2,1,0:T(8,128)(2,1)S(1)}, u32[]{:S(2)}, u32[]{:S(2)}) collective-permute-start(bf16[4,512,128]{2,1,0:T(8,128)(2,1)S(1)} %get-tuple-element.103), channel_id=1, source_target_pairs={{0,1},{1,0},{2,3},{3,2},{4,5},{5,4},{6,7},{7,6},{8,9},{9,8},{10,11... | collective-permute-start | bytes 1572872 | tf_op jit(solution)/shard_map/ppermute | solution.py:40
  67.0 5.9 %collective-permute-start.17 = (bf16[3,512,128]{2,1,0:T(8,128)(2,1)S(1)}, bf16[3,512,128]{2,1,0:T(8,128)(2,1)S(1)}, u32[]{:S(2)}, u32[]{:S(2)}) collective-permute-start(bf16[3,512,128]{2,1,0:T(8,128)(2,1)S(1)} %slice_bitcast_fusion.4), channel_id=1, source_target_pairs={{0,1},{1,0},{2,3},{3,2},{4,5},{5,4},{6,7},{7,6},{8,9},{9,8},{10,11... | collective-permute-start | bytes 1179656 | tf_op jit(solution)/shard_map/ppermute | solution.py:40
  69.6 13.6 %collective-permute-start.22 = (bf16[2,3,512,128]{3,2,1,0:T(8,128)(2,1)S(1)}, bf16[2,3,512,128]{3,2,1,0:T(8,128)(2,1)S(1)}, u32[]{:S(2)}, u32[]{:S(2)}) collective-permute-start(bf16[2,3,512,128]{3,2,1,0:T(8,128)(2,1)S(1)} %collective-permute-done.13.rest_16_), channel_id=1, source_target_pairs={{0,8},{1,57},{2,10},{3,59},{4,12},{5,61},{6,14},{7,63},{8,16},{9,1... | collective-permute-start | bytes 2359304 | tf_op jit(solution)/shard_map/ppermute | solution.py:31
  71.1 12.2 %collective-permute-start.24 = (bf16[2,3,512,128]{3,2,1,0:T(8,128)(2,1)S(1)}, bf16[2,3,512,128]{3,2,1,0:T(8,128)(2,1)S(1)}, u32[]{:S(2)}, u32[]{:S(2)}) collective-permute-start(bf16[2,3,512,128]{3,2,1,0:T(8,128)(2,1)S(1)} %shard_map.65), channel_id=1, source_target_pairs={{0,64},{1,193},{2,66},{3,195},{4,68},{5,197},{6,70},{7,199},{8,72}... | collective-permute-start | bytes 2359304 | tf_op jit(solution)/shard_map/ppermute | solution.py:31
  82.6 8.0 %collective-permute-start.18 = (bf16[3,448,512]{2,1,0:T(8,128)(2,1)S(1)}, bf16[3,448,512]{2,1,0:T(8,128)(2,1)S(1)}, u32[]{:S(2)}, u32[]{:S(2)}) collective-permute-start(bf16[3,448,512]{2,1,0:T(8,128)(2,1)S(1)} %shard_map.61), channel_id=1, source_target_pairs={{0,1},{1,0},{2,3},{3,2},{4,5},{5,4},{6,7},{7,6},{8,9},{9,8},{10,11... | collective-permute-start | bytes 4128776 | tf_op jit(solution)/shard_map/ppermute | solution.py:40
  83.2 12.9 %collective-permute-start.25 = (bf16[3,512,128]{2,1,0:T(8,128)(2,1)S(1)}, bf16[3,512,128]{2,1,0:T(8,128)(2,1)S(1)}, u32[]{:S(2)}, u32[]{:S(2)}) collective-permute-start(bf16[3,512,128]{2,1,0:T(8,128)(2,1)S(1)} %slice_bitcast_fusion.3), channel_id=1, source_target_pairs={{0,8},{1,57},{2,10},{3,59},{4,12},{5,61},{6,14},{7,63},{8,16},{9,1... | collective-permute-start | bytes 1179656 | tf_op jit(solution)/shard_map/ppermute | solution.py:31
  83.7 12.5 %collective-permute-start.26 = (bf16[3,512,128]{2,1,0:T(8,128)(2,1)S(1)}, bf16[3,512,128]{2,1,0:T(8,128)(2,1)S(1)}, u32[]{:S(2)}, u32[]{:S(2)}) collective-permute-start(bf16[3,512,128]{2,1,0:T(8,128)(2,1)S(1)} %slice_bitcast_fusion.2), channel_id=1, source_target_pairs={{0,64},{1,193},{2,66},{3,195},{4,68},{5,197},{6,70},{7,199},{8,72}... | collective-permute-start | bytes 1179656 | tf_op jit(solution)/shard_map/ppermute | solution.py:31
  87.7 8.5 %collective-permute-start.20 = (bf16[224,512]{1,0:T(8,128)(2,1)S(1)}, bf16[224,512]{1,0:T(8,128)(2,1)S(1)}, u32[]{:S(2)}, u32[]{:S(2)}) collective-permute-start(bf16[224,512]{1,0:T(8,128)(2,1)S(1)} %get-tuple-element.78), channel_id=1, source_target_pairs={{0,2},{1,3},{2,4},{3,5},{4,6},{5,7},{6,0},{7,1},{8,10},{9,11},{10,... | collective-permute-start | bytes 688136 | tf_op jit(solution)/shard_map/ppermute | solution.py:36
  89.0 7.1 %collective-permute-start.21 = (bf16[224,512]{1,0:T(8,128)(2,1)S(1)}, bf16[224,512]{1,0:T(8,128)(2,1)S(1)}, u32[]{:S(2)}, u32[]{:S(2)}) collective-permute-start(bf16[224,512]{1,0:T(8,128)(2,1)S(1)} %get-tuple-element.79), channel_id=1, source_target_pairs={{0,6},{1,7},{2,0},{3,1},{4,2},{5,3},{6,4},{7,5},{8,14},{9,15},{10,... | collective-permute-start | bytes 688136 | tf_op jit(solution)/shard_map/ppermute | solution.py:36
  96.2 4.2 %collective-permute-start.27 = (bf16[2,3,512,128]{3,2,1,0:T(8,128)(2,1)S(1)}, bf16[2,3,512,128]{3,2,1,0:T(8,128)(2,1)S(1)}, u32[]{:S(2)}, u32[]{:S(2)}) collective-permute-start(bf16[2,3,512,128]{3,2,1,0:T(8,128)(2,1)S(1)} %shard_map.66), channel_id=1, source_target_pairs={{0,1},{1,0},{2,3},{3,2},{4,5},{5,4},{6,7},{7,6},{8,9},{9,8},{10,11... | collective-permute-start | bytes 2359304 | tf_op jit(solution)/shard_map/ppermute | solution.py:40
  97.3 13.6 %collective-permute-start.28 = (bf16[448,512]{1,0:T(8,128)(2,1)S(1)}, bf16[448,512]{1,0:T(8,128)(2,1)S(1)}, u32[]{:S(2)}, u32[]{:S(2)}) collective-permute-start(bf16[448,512]{1,0:T(8,128)(2,1)S(1)} %get-tuple-element.91), channel_id=1, source_target_pairs={{0,2},{1,3},{2,4},{3,5},{4,6},{5,7},{6,0},{7,1},{8,10},{9,11},{10,... | collective-permute-start | bytes 1376264 | tf_op jit(solution)/shard_map/ppermute | solution.py:36
  98.7 12.2 %collective-permute-start.29 = (bf16[448,512]{1,0:T(8,128)(2,1)S(1)}, bf16[448,512]{1,0:T(8,128)(2,1)S(1)}, u32[]{:S(2)}, u32[]{:S(2)}) collective-permute-start(bf16[448,512]{1,0:T(8,128)(2,1)S(1)} %get-tuple-element.92), channel_id=1, source_target_pairs={{0,6},{1,7},{2,0},{3,1},{4,2},{5,3},{6,4},{7,5},{8,14},{9,15},{10,... | collective-permute-start | bytes 1376264 | tf_op jit(solution)/shard_map/ppermute | solution.py:36
  113.5 9.5 %collective-permute-start.30 = (bf16[3,576,512]{2,1,0:T(8,128)(2,1)S(1)}, bf16[3,576,512]{2,1,0:T(8,128)(2,1)S(1)}, u32[]{:S(2)}, u32[]{:S(2)}) collective-permute-start(bf16[3,576,512]{2,1,0:T(8,128)(2,1)S(1)} %shard_map.70), channel_id=1, source_target_pairs={{0,1},{1,0},{2,3},{3,2},{4,5},{5,4},{6,7},{7,6},{8,9},{9,8},{10,11... | collective-permute-start | bytes 5308424 | tf_op jit(solution)/shard_map/ppermute | solution.py:40
  119.8 10.1 %collective-permute-start.32 = (bf16[288,512]{1,0:T(8,128)(2,1)S(1)}, bf16[288,512]{1,0:T(8,128)(2,1)S(1)}, u32[]{:S(2)}, u32[]{:S(2)}) collective-permute-start(bf16[288,512]{1,0:T(8,128)(2,1)S(1)} %get-tuple-element.99), channel_id=1, source_target_pairs={{0,2},{1,3},{2,4},{3,5},{4,6},{5,7},{6,0},{7,1},{8,10},{9,11},{10,... | collective-permute-start | bytes 884744 | tf_op jit(solution)/shard_map/ppermute | solution.py:36
  120.9 9.0 %collective-permute-start.33 = (bf16[288,512]{1,0:T(8,128)(2,1)S(1)}, bf16[288,512]{1,0:T(8,128)(2,1)S(1)}, u32[]{:S(2)}, u32[]{:S(2)}) collective-permute-start(bf16[288,512]{1,0:T(8,128)(2,1)S(1)} %get-tuple-element.100), channel_id=1, source_target_pairs={{0,6},{1,7},{2,0},{3,1},{4,2},{5,3},{6,4},{7,5},{8,14},{9,15},{10,... | collective-permute-start | bytes 884744 | tf_op jit(solution)/shard_map/ppermute | solution.py:36
  130.1 15.2 %collective-permute-start.34 = (bf16[576,512]{1,0:T(8,128)(2,1)S(1)}, bf16[576,512]{1,0:T(8,128)(2,1)S(1)}, u32[]{:S(2)}, u32[]{:S(2)}) collective-permute-start(bf16[576,512]{1,0:T(8,128)(2,1)S(1)} %get-tuple-element.101), channel_id=1, source_target_pairs={{0,2},{1,3},{2,4},{3,5},{4,6},{5,7},{6,0},{7,1},{8,10},{9,11},{10,... | collective-permute-start | bytes 1769480 | tf_op jit(solution)/shard_map/ppermute | solution.py:36
  130.5 14.9 %collective-permute-start.35 = (bf16[576,512]{1,0:T(8,128)(2,1)S(1)}, bf16[576,512]{1,0:T(8,128)(2,1)S(1)}, u32[]{:S(2)}, u32[]{:S(2)}) collective-permute-start(bf16[576,512]{1,0:T(8,128)(2,1)S(1)} %get-tuple-element.102), channel_id=1, source_target_pairs={{0,6},{1,7},{2,0},{3,1},{4,2},{5,3},{6,4},{7,5},{8,14},{9,15},{10,... | collective-permute-start | bytes 1769480 | tf_op jit(solution)/shard_map/ppermute | solution.py:36
  (11 other events, 84.6 us)

commit v2 on v1

--- a/solution.py
+++ b/solution.py
@@ -299,7 +299,7 @@
                 arrays.append(array)
             places.setdefault(code, []).append((which, at, kv))
     _, suffix, width = queries.shape
-    batch = 4
+    batch = max(n for n in range(1, 8) if count % n == 0)
     vmem = pl.BlockSpec(memory_space=pltpu.VMEM)
     smem = pl.BlockSpec(memory_space=pltpu.SMEM)
     shape = jax.ShapeDtypeStruct((count, suffix, width), jnp.bfloat16)

time: 148 us -> 146 us (0.986)
  Pallas kernels: 35.7 us -> 33.7 us
    pallas_call x2, Pallas kernels: 14.3 us -> 12.3 us  [attend(): pl.pallas_call(functools.partial(attention_kernel, places, len(arrays), l...]
  transfers between devices with their start and end apart: 36 -> 36, of which waited for: 16 -> 17; matrix products, arithmetic and copies ran while one was open for 0% -> 0% of each run, Pallas kernels for 21% -> 20%
where the time goes in v2:
time: 146 us
  waiting for transfers between devices  62.8 us (43%)
  starting transfers between devices  47.3 us (32%)
  Pallas kernels  33.7 us (23%)
  local copies, waits for them, and re-layouts  1.84 us (1%)
    ppermute x14, waiting for transfers between devices, send_cache(): return lax.ppermute(value, ('cache', 'tensor'), pairs)  32.2 us
    ppermute x8, waiting for transfers between devices, send_y(): return lax.ppermute(value, 'tensor', pairs)  20.8 us
    ppermute x14, starting transfers between devices, send_cache(): return lax.ppermute(value, ('cache', 'tensor'), pairs)  19.7 us
    ppermute x14, starting transfers between devices, swap_core(): return lax.ppermute(value, 'tensor', [(t, t ^ 1) for t in range(2 * NY)])  16 us
    pallas_call x10, Pallas kernels, project(): pl.pallas_call(kernel, out_shape=out_shape, in_specs=[pl.BlockSpec(memory...  15.9 us
    pallas_call x2, Pallas kernels, attend(): pl.pallas_call(functools.partial(attention_kernel, places, len(arrays), l...  12.3 us
    ppermute x8, starting transfers between devices, send_y(): return lax.ppermute(value, 'tensor', pairs)  11.7 us
    ppermute x14, waiting for transfers between devices, swap_core(): return lax.ppermute(value, 'tensor', [(t, t ^ 1) for t in range(2 * NY)])  9.87 us
  transfers between devices with their start and end apart: 36, of which 17 were waited for; matrix products, arithmetic and copies ran while one was open for 0% of the time, Pallas kernels for 20%

profile of v2, /device:TPU:1, one launch (start us, length us, event | category | flops | bytes accessed | tf_op | source)
XLA Modules:
  0.0 145.9 jit_solution(17220032759792033118)
XLA Ops:
  0.0 3.2 %collective-permute-start = (bf16[2,512,128]{2,1,0:T(8,128)(2,1)}, bf16[2,512,128]{2,1,0:T(8,128)(2,1)S(1)}, u32[]{:S(2)}, u32[]{:S(2)}) collective-permute-start(bf16[2,512,128]{2,1,0:T(8,128)(2,1)} %bitcast.30), channel_id=1, source_target_pairs={{0,1},{1,0},{2,3},{3,2},{4,5},{5,4},{6,7},{7,6},{8,9},{9,8},{10,11... | collective-permute-start | bytes 786440 | tf_op jit(solution)/shard_map/ppermute | solution.py:40
  6.4 5.6 %collective-permute-start.2 = (bf16[2,2,512,128]{3,2,1,0:T(8,128)(2,1)S(1)}, bf16[2,2,512,128]{3,2,1,0:T(8,128)(2,1)S(1)}, u32[]{:S(2)}, u32[]{:S(2)}) collective-permute-start(bf16[2,2,512,128]{3,2,1,0:T(8,128)(2,1)S(1)} %shard_map.55), channel_id=1, source_target_pairs={{0,8},{1,57},{2,10},{3,59},{4,12},{5,61},{6,14},{7,63},{8,16},{9,1... | collective-permute-start | bytes 1572872 | tf_op jit(solution)/shard_map/ppermute | solution.py:31
  12.7 2.9 %shard_map.56 = (s32[32]{0:T(128)S(1)}, s32[32]{0:T(128)S(1)}, s32[2]{0:T(128)S(1)}) custom-call(s32[32]{0:T(128)S(1)} %bitcast.34), custom_call_target="tpu_custom_call" | custom-call | flops 1000 | bytes 1000 | tf_op jit(solution)/shard_map/pallas_call | solution.py:220
  15.6 2.5 %collective-permute-done.2.refs_0_.rest_4_ = bf16[2,2,512,128]{3,2,1,0:T(8,128)(2,1)S(1)} collective-permute-done((bf16[2,2,512,128]{3,2,1,0:T(8,128)(2,1)S(1)}, bf16[2,2,512,128]{3,2,1,0:T(8,128)(2,1)S(1)}, u32[]{:S(2)}, u32[]{:S(2)}) %collective-permute-start.2) | collective-permute-done | bytes 524320 | tf_op jit(solution)/shard_map/ppermute | solution.py:31
  18.7 3.1 %collective-permute-start.4 = (bf16[2,2,512,128]{3,2,1,0:T(8,128)(2,1)S(1)}, bf16[2,2,512,128]{3,2,1,0:T(8,128)(2,1)S(1)}, u32[]{:S(2)}, u32[]{:S(2)}) collective-permute-start(bf16[2,2,512,128]{3,2,1,0:T(8,128)(2,1)S(1)} %collective-permute-done.2.refs_0_.rest_4_), channel_id=1, source_target_pairs={{0,8},{1,57},{2,10},{3,59},{4,12},{5,61},{6,14},{7,63},{8,16},{9,1... | collective-permute-start | bytes 1572872 | tf_op jit(solution)/shard_map/ppermute | solution.py:31
  22.3 4.2 %collective-permute-done.3.refs_2_.rest_3_ = bf16[2,2,512,128]{3,2,1,0:T(8,128)(2,1)S(1)} collective-permute-done((bf16[2,2,512,128]{3,2,1,0:T(8,128)(2,1)S(1)}, bf16[2,2,512,128]{3,2,1,0:T(8,128)(2,1)S(1)}, u32[]{:S(2)}, u32[]{:S(2)}) %collective-permute-start.3) | collective-permute-done | bytes 524320 | tf_op jit(solution)/shard_map/ppermute | solution.py:31
  27.9 2.8 %collective-permute-start.7 = (bf16[2,2,512,128]{3,2,1,0:T(8,128)(2,1)S(1)}, bf16[2,2,512,128]{3,2,1,0:T(8,128)(2,1)S(1)}, u32[]{:S(2)}, u32[]{:S(2)}) collective-permute-start(bf16[2,2,512,128]{3,2,1,0:T(8,128)(2,1)S(1)} %collective-permute-done.4.refs_2_.rest_6_), channel_id=1, source_target_pairs={{0,1},{1,0},{2,3},{3,2},{4,5},{5,4},{6,7},{7,6},{8,9},{9,8},{10,11... | collective-permute-start | bytes 1572872 | tf_op jit(solution)/shard_map/ppermute | solution.py:40
  35.3 15.5 %collective-permute-done.10.rest_8_.refs_0_ = bf16[2,2,512,128]{3,2,1,0:T(8,128)(2,1)S(1)} collective-permute-done((bf16[2,2,512,128]{3,2,1,0:T(8,128)(2,1)S(1)}, bf16[2,2,512,128]{3,2,1,0:T(8,128)(2,1)S(1)}, u32[]{:S(2)}, u32[]{:S(2)}) %collective-permute-start.10) | collective-permute-done | bytes 524320 | tf_op jit(solution)/shard_map/ppermute | solution.py:31
  50.8 2.3 %collective-permute-start.14 = (bf16[2,2,512,128]{3,2,1,0:T(8,128)(2,1)S(1)}, bf16[2,2,512,128]{3,2,1,0:T(8,128)(2,1)S(1)}, u32[]{:S(2)}, u32[]{:S(2)}) collective-permute-start(bf16[2,2,512,128]{3,2,1,0:T(8,128)(2,1)S(1)} %collective-permute-done.10.rest_8_.refs_0_), channel_id=1, source_target_pairs={{0,1},{1,0},{2,3},{3,2},{4,5},{5,4},{6,7},{7,6},{8,9},{9,8},{10,11... | collective-permute-start | bytes 1572872 | tf_op jit(solution)/shard_map/ppermute | solution.py:40
  53.2 1.8 %collective-permute-start.12 = (bf16[4,512,128]{2,1,0:T(8,128)(2,1)S(1)}, bf16[4,512,128]{2,1,0:T(8,128)(2,1)S(1)}, u32[]{:S(2)}, u32[]{:S(2)}) collective-permute-start(bf16[4,512,128]{2,1,0:T(8,128)(2,1)S(1)} %get-tuple-element.104), channel_id=1, source_target_pairs={{0,64},{1,193},{2,66},{3,195},{4,68},{5,197},{6,70},{7,199},{8,72}... | collective-permute-start | bytes 1572872 | tf_op jit(solution)/shard_map/ppermute | solution.py:31
  55.1 3.5 %collective-permute-done.11.rest_10_.refs_2_ = bf16[2,512,128]{2,1,0:T(8,128)(2,1)S(1)} collective-permute-done((bf16[2,512,128]{2,1,0:T(8,128)(2,1)S(1)}, bf16[2,512,128]{2,1,0:T(8,128)(2,1)S(1)}, u32[]{:S(2)}, u32[]{:S(2)}) %collective-permute-start.11) | collective-permute-done | bytes 262176 | tf_op jit(solution)/shard_map/ppermute | solution.py:31
  58.6 2.2 %collective-permute-start.16 = (bf16[3,512,128]{2,1,0:T(8,128)(2,1)S(1)}, bf16[3,512,128]{2,1,0:T(8,128)(2,1)S(1)}, u32[]{:S(2)}, u32[]{:S(2)}) collective-permute-start(bf16[3,512,128]{2,1,0:T(8,128)(2,1)S(1)} %slice_bitcast_fusion.5), channel_id=1, source_target_pairs={{0,1},{1,0},{2,3},{3,2},{4,5},{5,4},{6,7},{7,6},{8,9},{9,8},{10,11... | collective-permute-start | bytes 1179656 | tf_op jit(solution)/shard_map/ppermute | solution.py:40
  62.1 4.9 %collective-permute-done.13.rest_16_ = bf16[2,3,512,128]{3,2,1,0:T(8,128)(2,1)S(1)} collective-permute-done((bf16[2,3,512,128]{3,2,1,0:T(8,128)(2,1)S(1)}, bf16[2,3,512,128]{3,2,1,0:T(8,128)(2,1)S(1)}, u32[]{:S(2)}, u32[]{:S(2)}) %collective-permute-start.13) | collective-permute-done | bytes 786464 | tf_op jit(solution)/shard_map/ppermute | solution.py:31
  67.0 2.4 %collective-permute-start.17 = (bf16[3,512,128]{2,1,0:T(8,128)(2,1)S(1)}, bf16[3,512,128]{2,1,0:T(8,128)(2,1)S(1)}, u32[]{:S(2)}, u32[]{:S(2)}) collective-permute-start(bf16[3,512,128]{2,1,0:T(8,128)(2,1)S(1)} %slice_bitcast_fusion.4), channel_id=1, source_target_pairs={{0,1},{1,0},{2,3},{3,2},{4,5},{5,4},{6,7},{7,6},{8,9},{9,8},{10,11... | collective-permute-start | bytes 1179656 | tf_op jit(solution)/shard_map/ppermute | solution.py:40
  71.1 1.8 %collective-permute-start.24 = (bf16[2,3,512,128]{3,2,1,0:T(8,128)(2,1)S(1)}, bf16[2,3,512,128]{3,2,1,0:T(8,128)(2,1)S(1)}, u32[]{:S(2)}, u32[]{:S(2)}) collective-permute-start(bf16[2,3,512,128]{3,2,1,0:T(8,128)(2,1)S(1)} %shard_map.65), channel_id=1, source_target_pairs={{0,64},{1,193},{2,66},{3,195},{4,68},{5,197},{6,70},{7,199},{8,72}... | collective-permute-start | bytes 2359304 | tf_op jit(solution)/shard_map/ppermute | solution.py:31
  72.9 5.3 %shard_map.59 = bf16[14,32,1024]{2,1,0:T(8,128)(2,1)S(1)} custom-call(s32[32]{0:T(128)S(1)} %get-tuple-element.82.order, s32[32]{0:T(128)S(1)} %get-tuple-element.59.codes, bf16[32,32,1024]{2,1,0:T(8,128)(2,1)S(1)} %copy-done, bf16[2,32,32,128]{3,2,1,0:T(8,128)(2,1)S(1)} %copy-done.3, bf16[2,512,128]{2,1,0:T(8,128)(2,1)S(1)} %bitcast.32, ...), custom_call_target="tpu_custom_call" | custom-call | flops 939524096 | bytes 8388608 | tf_op jit(solution)/shard_map/pallas_call | solution.py:306
  79.4 2.1 %shard_map.61 = bf16[3,448,512]{2,1,0:T(8,128)(2,1)S(1)} custom-call(s32[2]{0:T(128)S(1)} %get-tuple-element.58.place, bf16[448,1024]{1,0:T(8,128)(2,1)S(1)} %bitcast.26, bf16[1024,4096]{1,0:T(8,128)(2,1)S(1)} %bitcast.19), custom_call_target="tpu_custom_call" | custom-call | flops 1409286144 | bytes 4194304 | tf_op jit(solution)/shard_map/pallas_call | solution.py:357
  82.7 2.6 %collective-permute-start.26 = (bf16[3,512,128]{2,1,0:T(8,128)(2,1)S(1)}, bf16[3,512,128]{2,1,0:T(8,128)(2,1)S(1)}, u32[]{:S(2)}, u32[]{:S(2)}) collective-permute-start(bf16[3,512,128]{2,1,0:T(8,128)(2,1)S(1)} %slice_bitcast_fusion.2), channel_id=1, source_target_pairs={{0,64},{1,193},{2,66},{3,195},{4,68},{5,197},{6,70},{7,199},{8,72}... | collective-permute-start | bytes 1179656 | tf_op jit(solution)/shard_map/ppermute | solution.py:31
  88.0 1.5 %collective-permute-start.21 = (bf16[224,512]{1,0:T(8,128)(2,1)S(1)}, bf16[224,512]{1,0:T(8,128)(2,1)S(1)}, u32[]{:S(2)}, u32[]{:S(2)}) collective-permute-start(bf16[224,512]{1,0:T(8,128)(2,1)S(1)} %get-tuple-element.79), channel_id=1, source_target_pairs={{0,6},{1,7},{2,0},{3,1},{4,2},{5,3},{6,4},{7,5},{8,14},{9,15},{10,... | collective-permute-start | bytes 688136 | tf_op jit(solution)/shard_map/ppermute | solution.py:36
  89.6 1.7 %shard_map.63 = (bf16[448,512]{1,0:T(8,128)(2,1)S(1)}, bf16[448,512]{1,0:T(8,128)(2,1)S(1)}) custom-call(s32[2]{0:T(128)S(1)} %get-tuple-element.58.place, bf16[448,1024]{1,0:T(8,128)(2,1)S(1)} %bitcast.28, bf16[1024,4096]{1,0:T(8,128)(2,1)S(1)} %bitcast.19, bf16[3,448,512]{2,1,0:T(8,128)(2,1)S(1)} %collective-permute-done.18.came_ref), custom_call_target="tpu_custom_call" | custom-call | flops 939524096 | bytes 4194304 | tf_op jit(solution)/shard_map/pallas_call | solution.py:357
  91.2 3.9 %collective-permute-done.20.top = bf16[224,512]{1,0:T(8,128)(2,1)S(1)} collective-permute-done((bf16[224,512]{1,0:T(8,128)(2,1)S(1)}, bf16[224,512]{1,0:T(8,128)(2,1)S(1)}, u32[]{:S(2)}, u32[]{:S(2)}) %collective-permute-start.20) | collective-permute-done | bytes 229408 | tf_op jit(solution)/shard_map/ppermute | solution.py:36
  96.3 1.6 %collective-permute-start.28 = (bf16[448,512]{1,0:T(8,128)(2,1)S(1)}, bf16[448,512]{1,0:T(8,128)(2,1)S(1)}, u32[]{:S(2)}, u32[]{:S(2)}) collective-permute-start(bf16[448,512]{1,0:T(8,128)(2,1)S(1)} %get-tuple-element.91), channel_id=1, source_target_pairs={{0,2},{1,3},{2,4},{3,5},{4,6},{5,7},{6,0},{7,1},{8,10},{9,11},{10,... | collective-permute-start | bytes 1376264 | tf_op jit(solution)/shard_map/ppermute | solution.py:36
  99.4 7.0 %shard_map.67 = bf16[18,32,1024]{2,1,0:T(8,128)(2,1)S(1)} custom-call(s32[32]{0:T(128)S(1)} %get-tuple-element.82.order, s32[32]{0:T(128)S(1)} %get-tuple-element.59.codes, bf16[32,32,1024]{2,1,0:T(8,128)(2,1)S(1)} %copy-done, bf16[2,32,32,128]{3,2,1,0:T(8,128)(2,1)S(1)} %copy-done.3, bf16[2,512,128]{2,1,0:T(8,128)(2,1)S(1)} %bitcast.33, ...), custom_call_target="tpu_custom_call" | custom-call | flops 1207959552 | bytes 8388608 | tf_op jit(solution)/shard_map/pallas_call | solution.py:306
  107.8 2.3 %collective-permute-done.28.refs_1_ = bf16[448,512]{1,0:T(8,128)(2,1)S(1)} collective-permute-done((bf16[448,512]{1,0:T(8,128)(2,1)S(1)}, bf16[448,512]{1,0:T(8,128)(2,1)S(1)}, u32[]{:S(2)}, u32[]{:S(2)}) %collective-permute-start.28) | collective-permute-done | bytes 458784 | tf_op jit(solution)/shard_map/ppermute | solution.py:36
  110.1 2.5 %shard_map.70 = bf16[3,576,512]{2,1,0:T(8,128)(2,1)S(1)} custom-call(s32[2]{0:T(128)S(1)} %get-tuple-element.58.place, bf16[576,1024]{1,0:T(8,128)(2,1)S(1)} %bitcast.21, bf16[1024,4096]{1,0:T(8,128)(2,1)S(1)} %bitcast.19), custom_call_target="tpu_custom_call" | custom-call | flops 1811939328 | bytes 4194304 | tf_op jit(solution)/shard_map/pallas_call | solution.py:357
  113.6 4.1 %collective-permute-done.31.came_ref = bf16[1,576,512]{2,1,0:T(8,128)(2,1)S(1)} collective-permute-done((bf16[1,576,512]{2,1,0:T(8,128)(2,1)S(1)}, bf16[1,576,512]{2,1,0:T(8,128)(2,1)S(1)}, u32[]{:S(2)}, u32[]{:S(2)}) %collective-permute-start.31) | collective-permute-done | bytes 589856 | tf_op jit(solution)/shard_map/ppermute | solution.py:40
  120.1 1.8 %collective-permute-start.33 = (bf16[288,512]{1,0:T(8,128)(2,1)S(1)}, bf16[288,512]{1,0:T(8,128)(2,1)S(1)}, u32[]{:S(2)}, u32[]{:S(2)}) collective-permute-start(bf16[288,512]{1,0:T(8,128)(2,1)S(1)} %get-tuple-element.100), channel_id=1, source_target_pairs={{0,6},{1,7},{2,0},{3,1},{4,2},{5,3},{6,4},{7,5},{8,14},{9,15},{10,... | collective-permute-start | bytes 884744 | tf_op jit(solution)/shard_map/ppermute | solution.py:36
  121.9 1.9 %shard_map.72 = (bf16[576,512]{1,0:T(8,128)(2,1)S(1)}, bf16[576,512]{1,0:T(8,128)(2,1)S(1)}) custom-call(s32[2]{0:T(128)S(1)} %get-tuple-element.58.place, bf16[576,1024]{1,0:T(8,128)(2,1)S(1)} %bitcast.23, bf16[1024,4096]{1,0:T(8,128)(2,1)S(1)} %bitcast.19, bf16[3,576,512]{2,1,0:T(8,128)(2,1)S(1)} %collective-permute-done.30.came_ref), custom_call_target="tpu_custom_call" | custom-call | flops 1207959552 | bytes 4194304 | tf_op jit(solution)/shard_map/pallas_call | solution.py:357
  123.9 4.8 %collective-permute-done.32.top = bf16[288,512]{1,0:T(8,128)(2,1)S(1)} collective-permute-done((bf16[288,512]{1,0:T(8,128)(2,1)S(1)}, bf16[288,512]{1,0:T(8,128)(2,1)S(1)}, u32[]{:S(2)}, u32[]{:S(2)}) %collective-permute-start.32) | collective-permute-done | bytes 294944 | tf_op jit(solution)/shard_map/ppermute | solution.py:36
  129.5 2.1 %collective-permute-start.35 = (bf16[576,512]{1,0:T(8,128)(2,1)S(1)}, bf16[576,512]{1,0:T(8,128)(2,1)S(1)}, u32[]{:S(2)}, u32[]{:S(2)}) collective-permute-start(bf16[576,512]{1,0:T(8,128)(2,1)S(1)} %get-tuple-element.102), channel_id=1, source_target_pairs={{0,6},{1,7},{2,0},{3,1},{4,2},{5,3},{6,4},{7,5},{8,14},{9,15},{10,... | collective-permute-start | bytes 1769480 | tf_op jit(solution)/shard_map/ppermute | solution.py:36
  134.1 9.7 %collective-permute-done.34.refs_4_ = bf16[576,512]{1,0:T(8,128)(2,1)S(1)} collective-permute-done((bf16[576,512]{1,0:T(8,128)(2,1)S(1)}, bf16[576,512]{1,0:T(8,128)(2,1)S(1)}, u32[]{:S(2)}, u32[]{:S(2)}) %collective-permute-start.34) | collective-permute-done | bytes 589856 | tf_op jit(solution)/shard_map/ppermute | solution.py:36
  143.8 2.1 %shard_map.75 = bf16[32,32,512]{2,1,0:T(8,128)(2,1)} custom-call(s32[32]{0:T(128)S(1)} %get-tuple-element.82.order, bf16[448,512]{1,0:T(8,128)(2,1)S(1)} %shard_map.62.refs_0_, bf16[448,512]{1,0:T(8,128)(2,1)S(1)} %collective-permute-done.28.refs_1_, bf16[448,512]{1,0:T(8,128)(2,1)S(1)} %collective-permute-done.29.refs_2_, ...), custom_call_target="tpu_custom_call" | custom-call | tf_op jit(solution)/shard_map/pallas_call | solution.py:463
  (83 shorter events, 29.8 us)
Async XLA Ops:
  0.0 4.6 %collective-permute-start = (bf16[2,512,128]{2,1,0:T(8,128)(2,1)}, bf16[2,512,128]{2,1,0:T(8,128)(2,1)S(1)}, u32[]{:S(2)}, u32[]{:S(2)}) collective-permute-start(bf16[2,512,128]{2,1,0:T(8,128)(2,1)} %bitcast.30), channel_id=1, source_target_pairs={{0,1},{1,0},{2,3},{3,2},{4,5},{5,4},{6,7},{7,6},{8,9},{9,8},{10,11... | collective-permute-start | bytes 786440 | tf_op jit(solution)/shard_map/ppermute | solution.py:40
  5.6 10.0 %collective-permute-start.1 = (bf16[2,2,512,128]{3,2,1,0:T(8,128)(2,1)S(1)}, bf16[2,2,512,128]{3,2,1,0:T(8,128)(2,1)S(1)}, u32[]{:S(2)}, u32[]{:S(2)}) collective-permute-start(bf16[2,2,512,128]{3,2,1,0:T(8,128)(2,1)S(1)} %shard_map.55), channel_id=1, source_target_pairs={{0,64},{1,193},{2,66},{3,195},{4,68},{5,197},{6,70},{7,199},{8,72}... | collective-permute-start | bytes 1572872 | tf_op jit(solution)/shard_map/ppermute | solution.py:31
  6.4 11.7 %collective-permute-start.2 = (bf16[2,2,512,128]{3,2,1,0:T(8,128)(2,1)S(1)}, bf16[2,2,512,128]{3,2,1,0:T(8,128)(2,1)S(1)}, u32[]{:S(2)}, u32[]{:S(2)}) collective-permute-start(bf16[2,2,512,128]{3,2,1,0:T(8,128)(2,1)S(1)} %shard_map.55), channel_id=1, source_target_pairs={{0,8},{1,57},{2,10},{3,59},{4,12},{5,61},{6,14},{7,63},{8,16},{9,1... | collective-permute-start | bytes 1572872 | tf_op jit(solution)/shard_map/ppermute | solution.py:31
  18.1 8.3 %collective-permute-start.3 = (bf16[2,2,512,128]{3,2,1,0:T(8,128)(2,1)S(1)}, bf16[2,2,512,128]{3,2,1,0:T(8,128)(2,1)S(1)}, u32[]{:S(2)}, u32[]{:S(2)}) collective-permute-start(bf16[2,2,512,128]{3,2,1,0:T(8,128)(2,1)S(1)} %collective-permute-done.1.refs_0_.rest_1_), channel_id=1, source_target_pairs={{0,64},{1,193},{2,66},{3,195},{4,68},{5,197},{6,70},{7,199},{8,72}... | collective-permute-start | bytes 1572872 | tf_op jit(solution)/shard_map/ppermute | solution.py:31
  18.7 9.2 %collective-permute-start.4 = (bf16[2,2,512,128]{3,2,1,0:T(8,128)(2,1)S(1)}, bf16[2,2,512,128]{3,2,1,0:T(8,128)(2,1)S(1)}, u32[]{:S(2)}, u32[]{:S(2)}) collective-permute-start(bf16[2,2,512,128]{3,2,1,0:T(8,128)(2,1)S(1)} %collective-permute-done.2.refs_0_.rest_4_), channel_id=1, source_target_pairs={{0,8},{1,57},{2,10},{3,59},{4,12},{5,61},{6,14},{7,63},{8,16},{9,1... | collective-permute-start | bytes 1572872 | tf_op jit(solution)/shard_map/ppermute | solution.py:31
  21.8 6.1 %collective-permute-start.5 = (bf16[2,2,512,128]{3,2,1,0:T(8,128)(2,1)S(1)}, bf16[2,2,512,128]{3,2,1,0:T(8,128)(2,1)S(1)}, u32[]{:S(2)}, u32[]{:S(2)}) collective-permute-start(bf16[2,2,512,128]{3,2,1,0:T(8,128)(2,1)S(1)} %collective-permute-done.1.refs_0_.rest_1_), channel_id=1, source_target_pairs={{0,1},{1,0},{2,3},{3,2},{4,5},{5,4},{6,7},{7,6},{8,9},{9,8},{10,11... | collective-permute-start | bytes 1572872 | tf_op jit(solution)/shard_map/ppermute | solution.py:40
  21.8 6.1 %collective-permute-start.6 = (bf16[2,2,512,128]{3,2,1,0:T(8,128)(2,1)S(1)}, bf16[2,2,512,128]{3,2,1,0:T(8,128)(2,1)S(1)}, u32[]{:S(2)}, u32[]{:S(2)}) collective-permute-start(bf16[2,2,512,128]{3,2,1,0:T(8,128)(2,1)S(1)} %collective-permute-done.2.refs_0_.rest_4_), channel_id=1, source_target_pairs={{0,1},{1,0},{2,3},{3,2},{4,5},{5,4},{6,7},{7,6},{8,9},{9,8},{10,11... | collective-permute-start | bytes 1572872 | tf_op jit(solution)/shard_map/ppermute | solution.py:40
  27.9 4.3 %collective-permute-start.7 = (bf16[2,2,512,128]{3,2,1,0:T(8,128)(2,1)S(1)}, bf16[2,2,512,128]{3,2,1,0:T(8,128)(2,1)S(1)}, u32[]{:S(2)}, u32[]{:S(2)}) collective-permute-start(bf16[2,2,512,128]{3,2,1,0:T(8,128)(2,1)S(1)} %collective-permute-done.4.refs_2_.rest_6_), channel_id=1, source_target_pairs={{0,1},{1,0},{2,3},{3,2},{4,5},{5,4},{6,7},{7,6},{8,9},{9,8},{10,11... | collective-permute-start | bytes 1572872 | tf_op jit(solution)/shard_map/ppermute | solution.py:40
  32.3 18.4 %collective-permute-start.9 = (bf16[2,4,512,128]{3,2,1,0:T(8,128)(2,1)S(1)}, bf16[2,4,512,128]{3,2,1,0:T(8,128)(2,1)S(1)}, u32[]{:S(2)}, u32[]{:S(2)}) collective-permute-start(bf16[2,4,512,128]{3,2,1,0:T(8,128)(2,1)S(1)} %shard_map.58), channel_id=1, source_target_pairs={{0,64},{1,193},{2,66},{3,195},{4,68},{5,197},{6,70},{7,199},{8,72}... | collective-permute-start | bytes 3145736 | tf_op jit(solution)/shard_map/ppermute | solution.py:31
  33.9 16.8 %collective-permute-start.8 = (bf16[2,3,512,128]{3,2,1,0:T(8,128)(2,1)S(1)}, bf16[2,3,512,128]{3,2,1,0:T(8,128)(2,1)S(1)}, u32[]{:S(2)}, u32[]{:S(2)}) collective-permute-start(bf16[2,3,512,128]{3,2,1,0:T(8,128)(2,1)S(1)} %shard_map.57), channel_id=1, source_target_pairs={{0,8},{1,57},{2,10},{3,59},{4,12},{5,61},{6,14},{7,63},{8,16},{9,1... | collective-permute-start | bytes 2359304 | tf_op jit(solution)/shard_map/ppermute | solution.py:31
  34.5 16.2 %collective-permute-start.10 = (bf16[2,2,512,128]{3,2,1,0:T(8,128)(2,1)S(1)}, bf16[2,2,512,128]{3,2,1,0:T(8,128)(2,1)S(1)}, u32[]{:S(2)}, u32[]{:S(2)}) collective-permute-start(bf16[2,2,512,128]{3,2,1,0:T(8,128)(2,1)S(1)} %collective-permute-done.4.refs_2_.rest_6_), channel_id=1, source_target_pairs={{0,8},{1,57},{2,10},{3,59},{4,12},{5,61},{6,14},{7,63},{8,16},{9,1... | collective-permute-start | bytes 1572872 | tf_op jit(solution)/shard_map/ppermute | solution.py:31
  50.8 11.3 %collective-permute-start.14 = (bf16[2,2,512,128]{3,2,1,0:T(8,128)(2,1)S(1)}, bf16[2,2,512,128]{3,2,1,0:T(8,128)(2,1)S(1)}, u32[]{:S(2)}, u32[]{:S(2)}) collective-permute-start(bf16[2,2,512,128]{3,2,1,0:T(8,128)(2,1)S(1)} %collective-permute-done.10.rest_8_.refs_0_), channel_id=1, source_target_pairs={{0,1},{1,0},{2,3},{3,2},{4,5},{5,4},{6,7},{7,6},{8,9},{9,8},{10,11... | collective-permute-start | bytes 1572872 | tf_op jit(solution)/shard_map/ppermute | solution.py:40
  53.0 5.5 %collective-permute-start.11 = (bf16[2,512,128]{2,1,0:T(8,128)(2,1)S(1)}, bf16[2,512,128]{2,1,0:T(8,128)(2,1)S(1)}, u32[]{:S(2)}, u32[]{:S(2)}) collective-permute-start(bf16[2,512,128]{2,1,0:T(8,128)(2,1)S(1)} %slice_bitcast_fusion.6), channel_id=1, source_target_pairs={{0,8},{1,57},{2,10},{3,59},{4,12},{5,61},{6,14},{7,63},{8,16},{9,1... | collective-permute-start | bytes 786440 | tf_op jit(solution)/shard_map/ppermute | solution.py:31
  53.0 13.9 %collective-permute-start.13 = (bf16[2,3,512,128]{3,2,1,0:T(8,128)(2,1)S(1)}, bf16[2,3,512,128]{3,2,1,0:T(8,128)(2,1)S(1)}, u32[]{:S(2)}, u32[]{:S(2)}) collective-permute-start(bf16[2,3,512,128]{3,2,1,0:T(8,128)(2,1)S(1)} %collective-permute-done.8.rest_11_), channel_id=1, source_target_pairs={{0,8},{1,57},{2,10},{3,59},{4,12},{5,61},{6,14},{7,63},{8,16},{9,1... | collective-permute-start | bytes 2359304 | tf_op jit(solution)/shard_map/ppermute | solution.py:31
  53.2 8.9 %collective-permute-start.12 = (bf16[4,512,128]{2,1,0:T(8,128)(2,1)S(1)}, bf16[4,512,128]{2,1,0:T(8,128)(2,1)S(1)}, u32[]{:S(2)}, u32[]{:S(2)}) collective-permute-start(bf16[4,512,128]{2,1,0:T(8,128)(2,1)S(1)} %get-tuple-element.104), channel_id=1, source_target_pairs={{0,64},{1,193},{2,66},{3,195},{4,68},{5,197},{6,70},{7,199},{8,72}... | collective-permute-start | bytes 1572872 | tf_op jit(solution)/shard_map/ppermute | solution.py:31
  55.0 7.1 %collective-permute-start.15 = (bf16[4,512,128]{2,1,0:T(8,128)(2,1)S(1)}, bf16[4,512,128]{2,1,0:T(8,128)(2,1)S(1)}, u32[]{:S(2)}, u32[]{:S(2)}) collective-permute-start(bf16[4,512,128]{2,1,0:T(8,128)(2,1)S(1)} %get-tuple-element.103), channel_id=1, source_target_pairs={{0,1},{1,0},{2,3},{3,2},{4,5},{5,4},{6,7},{7,6},{8,9},{9,8},{10,11... | collective-permute-start | bytes 1572872 | tf_op jit(solution)/shard_map/ppermute | solution.py:40
  67.0 5.9 %collective-permute-start.17 = (bf16[3,512,128]{2,1,0:T(8,128)(2,1)S(1)}, bf16[3,512,128]{2,1,0:T(8,128)(2,1)S(1)}, u32[]{:S(2)}, u32[]{:S(2)}) collective-permute-start(bf16[3,512,128]{2,1,0:T(8,128)(2,1)S(1)} %slice_bitcast_fusion.4), channel_id=1, source_target_pairs={{0,1},{1,0},{2,3},{3,2},{4,5},{5,4},{6,7},{7,6},{8,9},{9,8},{10,11... | collective-permute-start | bytes 1179656 | tf_op jit(solution)/shard_map/ppermute | solution.py:40
  69.6 12.6 %collective-permute-start.22 = (bf16[2,3,512,128]{3,2,1,0:T(8,128)(2,1)S(1)}, bf16[2,3,512,128]{3,2,1,0:T(8,128)(2,1)S(1)}, u32[]{:S(2)}, u32[]{:S(2)}) collective-permute-start(bf16[2,3,512,128]{3,2,1,0:T(8,128)(2,1)S(1)} %collective-permute-done.13.rest_16_), channel_id=1, source_target_pairs={{0,8},{1,57},{2,10},{3,59},{4,12},{5,61},{6,14},{7,63},{8,16},{9,1... | collective-permute-start | bytes 2359304 | tf_op jit(solution)/shard_map/ppermute | solution.py:31
  71.1 11.2 %collective-permute-start.24 = (bf16[2,3,512,128]{3,2,1,0:T(8,128)(2,1)S(1)}, bf16[2,3,512,128]{3,2,1,0:T(8,128)(2,1)S(1)}, u32[]{:S(2)}, u32[]{:S(2)}) collective-permute-start(bf16[2,3,512,128]{3,2,1,0:T(8,128)(2,1)S(1)} %shard_map.65), channel_id=1, source_target_pairs={{0,64},{1,193},{2,66},{3,195},{4,68},{5,197},{6,70},{7,199},{8,72}... | collective-permute-start | bytes 2359304 | tf_op jit(solution)/shard_map/ppermute | solution.py:31
  81.6 8.0 %collective-permute-start.18 = (bf16[3,448,512]{2,1,0:T(8,128)(2,1)S(1)}, bf16[3,448,512]{2,1,0:T(8,128)(2,1)S(1)}, u32[]{:S(2)}, u32[]{:S(2)}) collective-permute-start(bf16[3,448,512]{2,1,0:T(8,128)(2,1)S(1)} %shard_map.61), channel_id=1, source_target_pairs={{0,1},{1,0},{2,3},{3,2},{4,5},{5,4},{6,7},{7,6},{8,9},{9,8},{10,11... | collective-permute-start | bytes 4128776 | tf_op jit(solution)/shard_map/ppermute | solution.py:40
  82.3 12.9 %collective-permute-start.25 = (bf16[3,512,128]{2,1,0:T(8,128)(2,1)S(1)}, bf16[3,512,128]{2,1,0:T(8,128)(2,1)S(1)}, u32[]{:S(2)}, u32[]{:S(2)}) collective-permute-start(bf16[3,512,128]{2,1,0:T(8,128)(2,1)S(1)} %slice_bitcast_fusion.3), channel_id=1, source_target_pairs={{0,8},{1,57},{2,10},{3,59},{4,12},{5,61},{6,14},{7,63},{8,16},{9,1... | collective-permute-start | bytes 1179656 | tf_op jit(solution)/shard_map/ppermute | solution.py:31
  82.7 12.5 %collective-permute-start.26 = (bf16[3,512,128]{2,1,0:T(8,128)(2,1)S(1)}, bf16[3,512,128]{2,1,0:T(8,128)(2,1)S(1)}, u32[]{:S(2)}, u32[]{:S(2)}) collective-permute-start(bf16[3,512,128]{2,1,0:T(8,128)(2,1)S(1)} %slice_bitcast_fusion.2), channel_id=1, source_target_pairs={{0,64},{1,193},{2,66},{3,195},{4,68},{5,197},{6,70},{7,199},{8,72}... | collective-permute-start | bytes 1179656 | tf_op jit(solution)/shard_map/ppermute | solution.py:31
  86.6 8.5 %collective-permute-start.20 = (bf16[224,512]{1,0:T(8,128)(2,1)S(1)}, bf16[224,512]{1,0:T(8,128)(2,1)S(1)}, u32[]{:S(2)}, u32[]{:S(2)}) collective-permute-start(bf16[224,512]{1,0:T(8,128)(2,1)S(1)} %get-tuple-element.78), channel_id=1, source_target_pairs={{0,2},{1,3},{2,4},{3,5},{4,6},{5,7},{6,0},{7,1},{8,10},{9,11},{10,... | collective-permute-start | bytes 688136 | tf_op jit(solution)/shard_map/ppermute | solution.py:36
  88.0 7.2 %collective-permute-start.21 = (bf16[224,512]{1,0:T(8,128)(2,1)S(1)}, bf16[224,512]{1,0:T(8,128)(2,1)S(1)}, u32[]{:S(2)}, u32[]{:S(2)}) collective-permute-start(bf16[224,512]{1,0:T(8,128)(2,1)S(1)} %get-tuple-element.79), channel_id=1, source_target_pairs={{0,6},{1,7},{2,0},{3,1},{4,2},{5,3},{6,4},{7,5},{8,14},{9,15},{10,... | collective-permute-start | bytes 688136 | tf_op jit(solution)/shard_map/ppermute | solution.py:36
  95.2 4.2 %collective-permute-start.27 = (bf16[2,3,512,128]{3,2,1,0:T(8,128)(2,1)S(1)}, bf16[2,3,512,128]{3,2,1,0:T(8,128)(2,1)S(1)}, u32[]{:S(2)}, u32[]{:S(2)}) collective-permute-start(bf16[2,3,512,128]{3,2,1,0:T(8,128)(2,1)S(1)} %shard_map.66), channel_id=1, source_target_pairs={{0,1},{1,0},{2,3},{3,2},{4,5},{5,4},{6,7},{7,6},{8,9},{9,8},{10,11... | collective-permute-start | bytes 2359304 | tf_op jit(solution)/shard_map/ppermute | solution.py:40
  96.3 13.8 %collective-permute-start.28 = (bf16[448,512]{1,0:T(8,128)(2,1)S(1)}, bf16[448,512]{1,0:T(8,128)(2,1)S(1)}, u32[]{:S(2)}, u32[]{:S(2)}) collective-permute-start(bf16[448,512]{1,0:T(8,128)(2,1)S(1)} %get-tuple-element.91), channel_id=1, source_target_pairs={{0,2},{1,3},{2,4},{3,5},{4,6},{5,7},{6,0},{7,1},{8,10},{9,11},{10,... | collective-permute-start | bytes 1376264 | tf_op jit(solution)/shard_map/ppermute | solution.py:36
  97.9 12.2 %collective-permute-start.29 = (bf16[448,512]{1,0:T(8,128)(2,1)S(1)}, bf16[448,512]{1,0:T(8,128)(2,1)S(1)}, u32[]{:S(2)}, u32[]{:S(2)}) collective-permute-start(bf16[448,512]{1,0:T(8,128)(2,1)S(1)} %get-tuple-element.92), channel_id=1, source_target_pairs={{0,6},{1,7},{2,0},{3,1},{4,2},{5,3},{6,4},{7,5},{8,14},{9,15},{10,... | collective-permute-start | bytes 1376264 | tf_op jit(solution)/shard_map/ppermute | solution.py:36
  112.7 9.2 %collective-permute-start.30 = (bf16[3,576,512]{2,1,0:T(8,128)(2,1)S(1)}, bf16[3,576,512]{2,1,0:T(8,128)(2,1)S(1)}, u32[]{:S(2)}, u32[]{:S(2)}) collective-permute-start(bf16[3,576,512]{2,1,0:T(8,128)(2,1)S(1)} %shard_map.70), channel_id=1, source_target_pairs={{0,1},{1,0},{2,3},{3,2},{4,5},{5,4},{6,7},{7,6},{8,9},{9,8},{10,11... | collective-permute-start | bytes 5308424 | tf_op jit(solution)/shard_map/ppermute | solution.py:40
  119.0 9.7 %collective-permute-start.32 = (bf16[288,512]{1,0:T(8,128)(2,1)S(1)}, bf16[288,512]{1,0:T(8,128)(2,1)S(1)}, u32[]{:S(2)}, u32[]{:S(2)}) collective-permute-start(bf16[288,512]{1,0:T(8,128)(2,1)S(1)} %get-tuple-element.99), channel_id=1, source_target_pairs={{0,2},{1,3},{2,4},{3,5},{4,6},{5,7},{6,0},{7,1},{8,10},{9,11},{10,... | collective-permute-start | bytes 884744 | tf_op jit(solution)/shard_map/ppermute | solution.py:36
  120.1 8.6 %collective-permute-start.33 = (bf16[288,512]{1,0:T(8,128)(2,1)S(1)}, bf16[288,512]{1,0:T(8,128)(2,1)S(1)}, u32[]{:S(2)}, u32[]{:S(2)}) collective-permute-start(bf16[288,512]{1,0:T(8,128)(2,1)S(1)} %get-tuple-element.100), channel_id=1, source_target_pairs={{0,6},{1,7},{2,0},{3,1},{4,2},{5,3},{6,4},{7,5},{8,14},{9,15},{10,... | collective-permute-start | bytes 884744 | tf_op jit(solution)/shard_map/ppermute | solution.py:36
  128.8 15.0 %collective-permute-start.34 = (bf16[576,512]{1,0:T(8,128)(2,1)S(1)}, bf16[576,512]{1,0:T(8,128)(2,1)S(1)}, u32[]{:S(2)}, u32[]{:S(2)}) collective-permute-start(bf16[576,512]{1,0:T(8,128)(2,1)S(1)} %get-tuple-element.101), channel_id=1, source_target_pairs={{0,2},{1,3},{2,4},{3,5},{4,6},{5,7},{6,0},{7,1},{8,10},{9,11},{10,... | collective-permute-start | bytes 1769480 | tf_op jit(solution)/shard_map/ppermute | solution.py:36
  129.5 14.3 %collective-permute-start.35 = (bf16[576,512]{1,0:T(8,128)(2,1)S(1)}, bf16[576,512]{1,0:T(8,128)(2,1)S(1)}, u32[]{:S(2)}, u32[]{:S(2)}) collective-permute-start(bf16[576,512]{1,0:T(8,128)(2,1)S(1)} %get-tuple-element.102), channel_id=1, source_target_pairs={{0,6},{1,7},{2,0},{3,1},{4,2},{5,3},{6,4},{7,5},{8,14},{9,15},{10,... | collective-permute-start | bytes 1769480 | tf_op jit(solution)/shard_map/ppermute | solution.py:36
  (11 other events, 82.5 us)
